TPU v7x, 32 devices: a whole 2x2x4 slice. The times are simulated.
32 devices in a mesh: sweep: 8 (over z, x), span: 4 (over y, core).
Axes of the slice: x: 2, y: 2, z: 4, core: 2. Of those that a mesh axis runs over, the one named last changes fastest.
Arguments:
- residual_in: float32 [8, 4, 4, 100, 128], P('sweep', 'span'), may hold values from -6 to 6
- diag_inverse: bfloat16 [8, 4, 100, 100, 128], P('sweep', 'span'), may hold values from -2 to 2
- up_block: bfloat16 [8, 4, 100, 100, 128], P('sweep', 'span'), may hold values from -0.4375 to 0.4375
- side_blocks: bfloat16 [8, 4, 3, 100, 100, 128], P('sweep', 'span'), may hold values from -1 to 1
- up_cols: int32 [8, 4, 128], P('sweep', 'span'), may hold values from 0 to 127, as said below
- down_cols: int32 [8, 4, 128], P('sweep', 'span'), may hold values from 0 to 127, as said below
- left_cols: int32 [8, 4, 128], P('sweep', 'span'), may hold values from 0 to 127, as said below
- right_cols: int32 [8, 4, 128], P('sweep', 'span'), may hold values from 0 to 127, as said below
Outputs:
- smoothed: float32 [8, 4, 4, 100, 128], P('sweep', 'span')
Inputs may be any that keep to these rules, and one draw needn't show every extreme that they name: For each slab and partition, a permutation of the 128 positions; down_cols of slab s is the inverse of up_cols of slab s + 1. `down_cols`: for each slab and partition, a permutation of the 128 positions. For each slab and partition, a permutation of the 128 positions; right_cols of partition p is the inverse of left_cols of partition p + 1. `right_cols`: for each slab and partition, a permutation of the 128 positions.
All inputs are finite; a program needn't handle non-finite values.
Results may differ from a plain program's by a relative error of at most 0.0003.
Values sent between devices are 32-bit elements; how exact they have to be, the bound alone decides.
No kernel may reach another device: no remote copies, remote signals or barrier semaphores. Data moves between devices by JAX's collectives and lax.ppermute only.
A program may use at most 128 MiB of HBM per device.

v0:
```python
import functools

import jax
import jax.numpy as jnp
from jax import lax
from jax.experimental import pallas as pl
from jax.experimental.pallas import tpu as pltpu
from jax.sharding import PartitionSpec as P

SUBLANES = 8
VMEM_LIMIT = 2 * 1024 * 1024
PREPARE_LIMIT = 12 * 1024 * 1024
LATERAL_START = 4
CHUNKS = 4
DIAG, UP, DOWN, LEFT, RIGHT = range(5)


def task_at(tick, place, count, vectors, choose=jnp.where):
    forward = ((tick - place) & 1) == 0
    rank = choose(forward, place, count - 1 - place)
    since = tick - rank - choose(forward, 0, count)
    late = since >= 2 * count
    since = choose(late, since - 2 * count, since)
    active = (since >= 0) & (since < 2 * vectors)
    half = choose(forward, 0, 1) + choose(late, 2, 0)
    return active, choose(active, since >> 1, 0), rank, forward, half


def turns(task):
    active, _, rank, _, half = task
    return active & (rank == 0) & (half > 0)


def lateral_plan(count, vectors):
    ticks = 4 * count + 2 * (vectors - 1)
    sent = [[None] * count for _ in range(ticks)]
    urgent = [[False] * count for _ in range(ticks)]
    for slab in range(count):
        left = ([], [])
        for half in range(3):
            rank = count - 1 - slab if half & 1 else slab
            for vector in range(vectors):
                made = 2 * vector + half * count + rank
                used = 2 * vector + (half + 1) * count + count - 1 - rank
                if used == made + 1:
                    sent[made][slab] = (1, (vector,))
                    urgent[made][slab] = True
                    continue
                left[1].append((used, made, vector))
                if used == made + 3:
                    sent[made + 1][slab] = (0, (vector,))
                else:
                    left[0].append((used, made, vector))
        for tick in range(LATERAL_START, ticks, 2):
            ready = [sorted(one for one in waiting if one[1] <= tick)[:2] for waiting in left]
            if not any(ready):
                continue
            pairs = 0 if ready[0] and (not ready[1] or ready[0][0][0] <= ready[1][0][0]) else 1
            assert tick <= ready[pairs][0][0] - 2
            sent[tick][slab] = (pairs, tuple(one[2] for one in ready[pairs]))
            for one in ready[pairs]:
                left[pairs].remove(one)
        assert not any(left)
    return sent, urgent


def numbers(plan, entry):
    if entry < 0:
        return [-1 if one is None else one[0] for one in plan]
    return [-1 if one is None or len(one[1]) <= entry else one[1][entry] for one in plan]


def pick(values, place):
    result = jnp.int32(values[0])
    for at, value in enumerate(values):
        if value != values[0]:
            result = jnp.where(place == at, value, result)
    return result


def product(matrix, vector, rows):
    count = matrix.shape[0]
    group = 3 * SUBLANES

    def add(first, amount, total):
        tile = vector[pl.ds(first, SUBLANES), :]
        for row in range(amount):
            total = total + matrix[first + row] * tile[row : row + 1, :]
        return total

    def body(step, total):
        for n in range(0, group, SUBLANES):
            total = add(pl.multiple_of(step * group + n, SUBLANES), SUBLANES, total)
        return total

    total = lax.fori_loop(0, count // group, body, jnp.zeros((rows, matrix.shape[2]), jnp.float32))
    for first in range(count - count % group, count, SUBLANES):
        total = add(first, min(SUBLANES, count - first), total)
    return total


def gathered(value, columns):
    index = jnp.broadcast_to(columns, value.shape)
    return jnp.take_along_axis(value, index, axis=1, mode="promise_in_bounds")


def take_lateral(base, vector, blocks, left_cols, right_cols, arrived, spare, pairs):
    part = lax.axis_index("span")
    on_right = (part & 1) == pairs

    @pl.when(jnp.where(on_right, part < lax.axis_size("span") - 1, part > 0))
    def _():
        spare[...] = gathered(arrived, jnp.where(on_right, right_cols[...], left_cols[...]))
        base[vector] = base[vector] - product(blocks.at[jnp.where(on_right, RIGHT, LEFT)], spare, spare.shape[0])


def prepare(block, ready, narrow, wide, sems):
    size, _, lanes = block.shape
    rows = ready.shape[1]
    share = size // CHUNKS
    copies = [
        pltpu.make_async_copy(block.at[pl.ds(n * share, share)], narrow.at[pl.ds(n * share, share)], sems.at[n])
        for n in range(CHUNKS)
    ]
    for copy in copies:
        copy.start()
    wide[pl.ds(size * rows, (rows - size) * rows), :] = jnp.zeros(((rows - size) * rows, lanes), jnp.float32)

    def widen(i, _):
        wide[pl.ds(pl.multiple_of(i * rows, SUBLANES), size), :] = narrow[i].astype(jnp.float32)
        return 0

    for n, copy in enumerate(copies):
        copy.wait()
        lax.fori_loop(n * share, (n + 1) * share, widen, 0, unroll=5)

    def turn(j, _):
        for i in range(0, rows, SUBLANES):
            ready[j, pl.ds(i, SUBLANES), :] = wide[pl.ds(i * rows + j, SUBLANES, stride=rows), :]
        return 0

    lax.fori_loop(0, size, turn, 0, unroll=4)


def first_kernel(block, residual, *refs):
    hbm_columns, (blocks, base, source, blank, *columns), (narrow, wide, sems, column_sems) = (
        refs[:4], refs[4:12], refs[12:]
    )
    copies = [
        pltpu.make_async_copy(there, here, column_sems.at[n])
        for n, (there, here) in enumerate(zip(hbm_columns, columns))
    ]
    for copy in copies:
        copy.start()
    prepare(block, blocks.at[DIAG], narrow, wide, sems)
    vectors, size, lanes = residual.shape
    rows = base.shape[1]
    base[:, pl.ds(rows - SUBLANES, SUBLANES), :] = jnp.zeros((vectors, SUBLANES, lanes), jnp.float32)
    base[:, pl.ds(0, size), :] = residual[...]
    source[...] = base[...]
    blank[...] = jnp.zeros_like(blank)
    for copy in copies:
        copy.wait()


def later_kernel(face, slot, block, blocks_in, blocks, narrow, wide, sems):
    prepare(block.at[(0,) * (len(block.shape) - 4) + (face,)], blocks.at[slot], narrow, wide, sems)


def task_kernel(
    tick, tasks, sent, columns_and_inputs, kept, values, spare
):
    up_cols, down_cols, left_cols, right_cols, source, incoming, arrived = columns_and_inputs
    value, *cross = values
    blocks, base, latest, out = kept
    rows = spare.shape[0]
    vectors, size, _ = out.shape
    place = lax.axis_index("sweep")
    task = task_at(tick, place, lax.axis_size("sweep"), vectors)
    active, vector, rank, forward, half = task

    if any(turns(one) for one in tasks):

        @pl.when(turns(task))
        def _():
            take_lateral(base, vector, blocks, left_cols, right_cols, arrived[0], spare, 1)

    @pl.when(active)
    def _():
        known = base[vector]
        value[...] = known
        base[vector] = source[vector]

        if any(one[0] and one[2] > 0 for one in tasks):

            @pl.when(rank > 0)
            def _():
                spare[...] = gathered(incoming[...], jnp.where(forward, up_cols[...], down_cols[...]))
                term = product(blocks.at[jnp.where(forward, UP, DOWN)], spare, rows)
                value[...] = known - term
                base[vector] = source[vector] - term

        spare[...] = value[...]
        fresh = product(blocks.at[DIAG], spare, rows)
        value[...] = fresh
        latest[vector] = fresh

        if any(one[0] and one[4] == 3 for one in tasks):

            @pl.when(half == 3)
            def _():
                out[vector] = fresh[:size]

    if cross:
        fill(cross[0], latest, sent, place)


def fill(cross, latest, plan, place):
    for entry in range(cross.shape[0]):
        chosen = numbers(plan, entry)
        if any(one >= 0 for one in chosen):
            vector = pick(chosen, place)

            @pl.when(vector >= 0)
            def _():
                cross[entry] = latest[vector]


def side_kernel(came, plan, columns_and_inputs, kept, values, spare):
    left_cols, right_cols, *arrived = columns_and_inputs
    blocks, base, latest = kept
    place = lax.axis_index("sweep")
    if values:
        fill(values[0], latest, plan, place)
    if arrived:
        pairs = pick(numbers(came, -1), place)
        for entry in range(arrived[0].shape[0]):
            chosen = numbers(came, entry)
            if any(one >= 0 for one in chosen):
                vector = pick(chosen, place)

                @pl.when(vector >= 0)
                def _():
                    take_lateral(
                        base, vector, blocks, left_cols, right_cols, arrived[0][entry], spare, pairs
                    )


def turn_kernel(tick, vectors, columns_and_inputs, kept, values, spare):
    left_cols, right_cols, incoming = columns_and_inputs
    blocks, base = kept
    task = task_at(tick, lax.axis_index("sweep"), lax.axis_size("sweep"), vectors)

    @pl.when(turns(task))
    def _():
        take_lateral(base, task[1], blocks, left_cols, right_cols, incoming[...], spare, 0)


def in_vmem(count):
    return [pl.BlockSpec(memory_space=pltpu.VMEM)] * count


def far(array):
    return pltpu.with_memory_space_constraint(array, pltpu.HBM)


def held(shape):
    return pltpu.VMEM(shape, jnp.float32)


def call(kernel, name, fixed, kept, fresh, spare):
    def body(*refs):
        inputs, outputs = refs[: len(fixed)], refs[len(fixed) + len(kept) : -1]
        kernel(inputs, outputs[: len(kept)], outputs[len(kept) :], refs[-1])

    return pl.pallas_call(
        body,
        out_shape=tuple(held(shape) for shape in [*(a.shape for a in kept), *fresh]),
        in_specs=in_vmem(len(fixed) + len(kept)),
        out_specs=tuple(in_vmem(len(fresh) + len(kept))),
        scratch_shapes=[held(spare)],
        input_output_aliases={len(fixed) + n: n for n in range(len(kept))},
        compiler_params=pltpu.CompilerParams(vmem_limit_bytes=VMEM_LIMIT),
        name=name,
    )(*fixed, *kept)


def preparing(size, rows, lanes):
    return [
        pltpu.VMEM((size, size, lanes), jnp.bfloat16),
        held((rows * rows, lanes)),
        pltpu.SemaphoreType.DMA((CHUNKS,)),
    ]


def first_call(block, residual, columns, rows):
    vectors, size, lanes = residual.shape
    several = (vectors, rows, lanes)
    in_hbm = pl.BlockSpec(memory_space=pltpu.HBM)
    return pl.pallas_call(
        first_kernel,
        out_shape=(
            held((5, size, rows, lanes)), held(several), held(several), held((rows, lanes)),
            *(pltpu.VMEM(one.shape, one.dtype) for one in columns),
        ),
        in_specs=[in_hbm, *in_vmem(1), *[in_hbm] * 4],
        out_specs=tuple(in_vmem(8)),
        scratch_shapes=[*preparing(size, rows, lanes), pltpu.SemaphoreType.DMA((4,))],
        compiler_params=pltpu.CompilerParams(vmem_limit_bytes=PREPARE_LIMIT),
        name="first",
    )(far(block), residual, *(far(one) for one in columns))


def later_call(block, face, slot, blocks):
    return pl.pallas_call(
        functools.partial(later_kernel, face, slot),
        out_shape=held(blocks.shape),
        in_specs=[pl.BlockSpec(memory_space=pltpu.HBM), *in_vmem(1)],
        out_specs=in_vmem(1)[0],
        scratch_shapes=preparing(*blocks.shape[1:]),
        input_output_aliases={1: 0},
        compiler_params=pltpu.CompilerParams(vmem_limit_bytes=PREPARE_LIMIT),
        name="later",
    )(far(block), blocks)


def per_device(
    residual_in, diag_inverse, up_block, side_blocks, up_cols, down_cols, left_cols, right_cols
):
    vectors, size, lanes = residual_in.shape[2:]
    rows = size + -size % SUBLANES
    columns = [one.reshape(1, lanes) for one in (up_cols, down_cols, left_cols, right_cols)]
    count = lax.axis_size("sweep")
    parts = lax.axis_size("span")
    ticks = 4 * count + 2 * (vectors - 1)
    sent, urgent = lateral_plan(count, vectors)
    even_pairs = [(p, p + 1) for p in range(0, parts - 1, 2)]
    odd_pairs = [(p, p + 1) for p in range(1, parts - 1, 2)]

    def closed(pairs, members):
        alone = [one for one in members if all(one not in two for two in pairs)]
        return [*pairs, *((b, a) for a, b in pairs), *((one, one) for one in alone)]

    def device(slab, part):
        return slab * parts + part

    blocks, base, source, blank, *columns = first_call(diag_inverse[0, 0], residual_in[0, 0], columns, rows)
    latest, out = pl.pallas_call(
        lambda *refs: None,
        out_shape=(held((vectors, rows, lanes)), held((vectors, size, lanes))),
        out_specs=tuple(in_vmem(2)),
        name="room",
    )()
    incoming = arrived = blank
    late_blocks = [(up_block, 0, UP), *((side_blocks, face, DOWN + face) for face in range(3))]

    def tasks_at(tick):
        return [task_at(tick, place, count, vectors, lambda which, a, b: a if which else b) for place in range(count)]

    for tick in range(ticks):
        tasks = tasks_at(tick)
        plan = sent[tick]
        turning = any(turns(one) for one in tasks)
        at_once = any(plan) and tick & 1 == 1
        blocks, base, latest, out, value, *cross = call(
            functools.partial(task_kernel, tick, tasks, plan),
            "task",
            (*columns, source, incoming, arrived if turning else blank),
            (blocks, base, latest, out),
            ((rows, lanes), *([(1, rows, lanes)] if at_once else [])),
            (rows, lanes),
        )

        if any(urgent[tick]) or any(one[0] and one[2] > 0 for one in tasks_at(tick + 1)):
            pairs = []
            swap = [(s, s + 1) for s in range(tick & 1, count - 1, 2)]
            for a, b in swap:
                forth, back = (0 if tasks[one][0] else 1 for one in (a, b))
                if forth and back:
                    forth = back = 0
                for p in range(parts):
                    pairs += [(device(a, p), device(b, p ^ forth)), (device(b, p), device(a, p ^ back))]
            alone = [s for s in range(count) if all(s not in two for two in swap)]
            pairs += [(device(s, x), device(s, y)) for s in alone for a, b in even_pairs for x, y in ((a, b), (b, a))]
            incoming = lax.ppermute(value, ("sweep", "span"), pairs)
        came = [None if not tick or urgent[tick - 1][s] else sent[tick - 1][s] for s in range(count)]
        later = any(plan) and not at_once
        if any(came) or later:
            blocks, base, latest, *made = call(
                functools.partial(side_kernel, came, plan),
                "side",
                (columns[2], columns[3], *([arrived] if any(came) else [])),
                (blocks, base, latest),
                ((2, rows, lanes),) if later else (),
                (rows, lanes),
            )
            cross += made
        if any(plan):
            pairs = [
                (device(s, a), device(s, b))
                for s in range(count)
                if plan[s] is not None
                for a, b in (odd_pairs if plan[s][0] else even_pairs)
            ]
            arrived = lax.ppermute(cross[0], ("sweep", "span"), closed(pairs, range(count * parts)))
        if any(urgent[tick]):
            blocks, base = call(
                functools.partial(turn_kernel, tick + 1, vectors),
                "turn",
                (columns[2], columns[3], incoming),
                (blocks, base),
                (),
                (rows, lanes),
            )
        if tick < len(late_blocks):
            blocks = later_call(*late_blocks[tick], blocks)
    return out[None, None]


def solution(mesh):
    return jax.shard_map(
        per_device,
        mesh=mesh,
        in_specs=(
            P("sweep", "span", None, None, None),
            P("sweep", "span", None, None, None),
            P("sweep", "span", None, None, None),
            P("sweep", "span", None, None, None, None),
            P("sweep", "span", None),
            P("sweep", "span", None),
            P("sweep", "span", None),
            P("sweep", "span", None),
        ),
        out_specs=P("sweep", "span", None, None, None),
        check_vma=False,
    )
```

profile of v0, /device:TPU:0, one launch (start us, length us, event | category | flops | bytes accessed | tf_op | source)
XLA Modules:
  0.0 194.5 jit_solution(14738265085266940488)
XLA Ops:
  0.9 3.0 %first.1 = (f32[5,100,104,128]{3,2,1,0:T(8,128)S(1)}, f32[4,104,128]{2,1,0:T(8,128)S(1)}, f32[4,104,128]{2,1,0:T(8,128)S(1)}, f32[104,128]{1,0:T(8,128)S(1)}, s3...) custom-call(bf16[100,100,128]{2,1,0:T(8,128)(2,1)} %bitcast.11, ...), custom_call_target="tpu_custom_call" | custom-call | tf_op jit(solution)/shard_map/first/pallas_call | solution.py:300
  10.1 2.9 %later.5.refs_7_ = f32[5,100,104,128]{3,2,1,0:T(8,128)S(1)} custom-call(bf16[1,1,3,100,100,128]{5,4,3,2,1,0:T(8,128)(2,1)} %block.7, f32[5,100,104,128]{3,2,1,0:T(8,128)S(1)} %get-tuple-element.351.blocks_in), custom_call_target="tpu_custom_call", output_to_operand_aliasing={{}: (1, {})} | custom-call | tf_op jit(solution)/shard_map/later/pallas_call | solution.py:315
  13.4 3.2 %collective-permute-start.2 = (f32[104,128]{1,0:T(8,128)S(1)}, f32[104,128]{1,0:T(8,128)S(1)}, u32[]{:S(2)}, u32[]{:S(2)}) collective-permute-start(f32[104,128]{1,0:T(8,128)S(1)} %get-tuple-element.355), channel_id=1, source_target_pairs={{0,4},{4,1},{1,5},{5,0},{2,6},{6,3},{3,7},{7,2},{8,12},{12,9},{9,1... | collective-permute-start | bytes 159752 | tf_op jit(solution)/shard_map/ppermute | solution.py:385
  19.6 2.9 %later.7.refs_7_ = f32[5,100,104,128]{3,2,1,0:T(8,128)S(1)} custom-call(bf16[1,1,3,100,100,128]{5,4,3,2,1,0:T(8,128)(2,1)} %block.7, f32[5,100,104,128]{3,2,1,0:T(8,128)S(1)} %get-tuple-element.361.blocks_in), custom_call_target="tpu_custom_call", output_to_operand_aliasing={{}: (1, {})} | custom-call | tf_op jit(solution)/shard_map/later/pallas_call | solution.py:315
  22.9 3.2 %collective-permute-start.4 = (f32[104,128]{1,0:T(8,128)S(1)}, f32[104,128]{1,0:T(8,128)S(1)}, u32[]{:S(2)}, u32[]{:S(2)}) collective-permute-start(f32[104,128]{1,0:T(8,128)S(1)} %get-tuple-element.365), channel_id=1, source_target_pairs={{0,4},{4,1},{1,5},{5,0},{2,6},{6,3},{3,7},{7,2},{8,12},{12,9},{9,1... | collective-permute-start | bytes 159752 | tf_op jit(solution)/shard_map/ppermute | solution.py:385
  30.7 4.9 %collective-permute-start.7 = (f32[104,128]{1,0:T(8,128)S(1)}, f32[104,128]{1,0:T(8,128)S(1)}, u32[]{:S(2)}, u32[]{:S(2)}) collective-permute-start(f32[104,128]{1,0:T(8,128)S(1)} %get-tuple-element.382), channel_id=1, source_target_pairs={{0,4},{4,1},{1,5},{5,0},{2,6},{6,3},{3,7},{7,2},{8,12},{12,9},{9,1... | collective-permute-start | bytes 159752 | tf_op jit(solution)/shard_map/ppermute | solution.py:385
  40.7 4.8 %collective-permute-start.11 = (f32[104,128]{1,0:T(8,128)S(1)}, f32[104,128]{1,0:T(8,128)S(1)}, u32[]{:S(2)}, u32[]{:S(2)}) collective-permute-start(f32[104,128]{1,0:T(8,128)S(1)} %get-tuple-element.402), channel_id=1, source_target_pairs={{0,4},{4,0},{1,5},{5,1},{2,6},{6,2},{3,7},{7,3},{8,12},{12,9},{9,1... | collective-permute-start | bytes 159752 | tf_op jit(solution)/shard_map/ppermute | solution.py:385
  49.8 4.9 %collective-permute-start.15 = (f32[104,128]{1,0:T(8,128)S(1)}, f32[104,128]{1,0:T(8,128)S(1)}, u32[]{:S(2)}, u32[]{:S(2)}) collective-permute-start(f32[104,128]{1,0:T(8,128)S(1)} %get-tuple-element.422), channel_id=1, source_target_pairs={{0,4},{4,0},{1,5},{5,1},{2,6},{6,2},{3,7},{7,3},{8,12},{12,8},{9,1... | collective-permute-start | bytes 159752 | tf_op jit(solution)/shard_map/ppermute | solution.py:385
  59.4 4.9 %collective-permute-start.19 = (f32[104,128]{1,0:T(8,128)S(1)}, f32[104,128]{1,0:T(8,128)S(1)}, u32[]{:S(2)}, u32[]{:S(2)}) collective-permute-start(f32[104,128]{1,0:T(8,128)S(1)} %get-tuple-element.442), channel_id=1, source_target_pairs={{0,4},{4,0},{1,5},{5,1},{2,6},{6,2},{3,7},{7,3},{8,13},{12,8},{9,1... | collective-permute-start | bytes 159752 | tf_op jit(solution)/shard_map/ppermute | solution.py:385
  67.7 6.5 %collective-permute-start.23 = (f32[104,128]{1,0:T(8,128)S(1)}, f32[104,128]{1,0:T(8,128)S(1)}, u32[]{:S(2)}, u32[]{:S(2)}) collective-permute-start(f32[104,128]{1,0:T(8,128)S(1)} %get-tuple-element.462), channel_id=1, source_target_pairs={{0,5},{4,0},{1,4},{5,1},{2,7},{6,2},{3,6},{7,3},{8,13},{12,8},{9,1... | collective-permute-start | bytes 159752 | tf_op jit(solution)/shard_map/ppermute | solution.py:385
  80.7 6.7 %collective-permute-start.27 = (f32[104,128]{1,0:T(8,128)S(1)}, f32[104,128]{1,0:T(8,128)S(1)}, u32[]{:S(2)}, u32[]{:S(2)}) collective-permute-start(f32[104,128]{1,0:T(8,128)S(1)} %get-tuple-element.482), channel_id=1, source_target_pairs={{0,4},{4,0},{1,5},{5,1},{2,6},{6,2},{3,7},{7,3},{8,13},{12,8},{9,1... | collective-permute-start | bytes 159752 | tf_op jit(solution)/shard_map/ppermute | solution.py:385
  92.9 5.6 %collective-permute-start.31 = (f32[104,128]{1,0:T(8,128)S(1)}, f32[104,128]{1,0:T(8,128)S(1)}, u32[]{:S(2)}, u32[]{:S(2)}) collective-permute-start(f32[104,128]{1,0:T(8,128)S(1)} %get-tuple-element.502), channel_id=1, source_target_pairs={{0,4},{4,0},{1,5},{5,1},{2,6},{6,2},{3,7},{7,3},{8,12},{12,8},{9,1... | collective-permute-start | bytes 159752 | tf_op jit(solution)/shard_map/ppermute | solution.py:385
  104.9 4.6 %collective-permute-start.35 = (f32[104,128]{1,0:T(8,128)S(1)}, f32[104,128]{1,0:T(8,128)S(1)}, u32[]{:S(2)}, u32[]{:S(2)}) collective-permute-start(f32[104,128]{1,0:T(8,128)S(1)} %get-tuple-element.522), channel_id=1, source_target_pairs={{0,4},{4,0},{1,5},{5,1},{2,6},{6,2},{3,7},{7,3},{8,12},{12,9},{9,1... | collective-permute-start | bytes 159752 | tf_op jit(solution)/shard_map/ppermute | solution.py:385
  116.1 3.1 %collective-permute-start.39 = (f32[104,128]{1,0:T(8,128)S(1)}, f32[104,128]{1,0:T(8,128)S(1)}, u32[]{:S(2)}, u32[]{:S(2)}) collective-permute-start(f32[104,128]{1,0:T(8,128)S(1)} %get-tuple-element.542), channel_id=1, source_target_pairs={{0,4},{4,1},{1,5},{5,0},{2,6},{6,3},{3,7},{7,2},{8,12},{12,9},{9,1... | collective-permute-start | bytes 159752 | tf_op jit(solution)/shard_map/ppermute | solution.py:385
  124.3 5.0 %collective-permute-start.43 = (f32[104,128]{1,0:T(8,128)S(1)}, f32[104,128]{1,0:T(8,128)S(1)}, u32[]{:S(2)}, u32[]{:S(2)}) collective-permute-start(f32[104,128]{1,0:T(8,128)S(1)} %get-tuple-element.562), channel_id=1, source_target_pairs={{0,4},{4,0},{1,5},{5,1},{2,6},{6,2},{3,7},{7,3},{8,12},{12,9},{9,1... | collective-permute-start | bytes 159752 | tf_op jit(solution)/shard_map/ppermute | solution.py:385
  133.1 5.5 %collective-permute-start.47 = (f32[104,128]{1,0:T(8,128)S(1)}, f32[104,128]{1,0:T(8,128)S(1)}, u32[]{:S(2)}, u32[]{:S(2)}) collective-permute-start(f32[104,128]{1,0:T(8,128)S(1)} %get-tuple-element.582), channel_id=1, source_target_pairs={{0,4},{4,0},{1,5},{5,1},{2,6},{6,2},{3,7},{7,3},{8,12},{12,8},{9,1... | collective-permute-start | bytes 159752 | tf_op jit(solution)/shard_map/ppermute | solution.py:385
  141.9 5.8 %collective-permute-start.51 = (f32[104,128]{1,0:T(8,128)S(1)}, f32[104,128]{1,0:T(8,128)S(1)}, u32[]{:S(2)}, u32[]{:S(2)}) collective-permute-start(f32[104,128]{1,0:T(8,128)S(1)} %get-tuple-element.602), channel_id=1, source_target_pairs={{0,4},{4,0},{1,5},{5,1},{2,6},{6,2},{3,7},{7,3},{8,13},{12,8},{9,1... | collective-permute-start | bytes 159752 | tf_op jit(solution)/shard_map/ppermute | solution.py:385
  151.1 6.2 %collective-permute-start.55 = (f32[104,128]{1,0:T(8,128)S(1)}, f32[104,128]{1,0:T(8,128)S(1)}, u32[]{:S(2)}, u32[]{:S(2)}) collective-permute-start(f32[104,128]{1,0:T(8,128)S(1)} %get-tuple-element.622), channel_id=1, source_target_pairs={{0,5},{4,0},{1,4},{5,1},{2,7},{6,2},{3,6},{7,3},{8,13},{12,8},{9,1... | collective-permute-start | bytes 159752 | tf_op jit(solution)/shard_map/ppermute | solution.py:385
  162.5 5.8 %collective-permute-start.58 = (f32[104,128]{1,0:T(8,128)S(1)}, f32[104,128]{1,0:T(8,128)S(1)}, u32[]{:S(2)}, u32[]{:S(2)}) collective-permute-start(f32[104,128]{1,0:T(8,128)S(1)} %get-tuple-element.639), channel_id=1, source_target_pairs={{0,5},{4,0},{1,4},{5,1},{2,7},{6,2},{3,6},{7,3},{8,13},{12,8},{9,1... | collective-permute-start | bytes 159752 | tf_op jit(solution)/shard_map/ppermute | solution.py:385
  168.3 3.0 %collective-permute-done.58.refs_5_ = f32[104,128]{1,0:T(8,128)S(1)} collective-permute-done((f32[104,128]{1,0:T(8,128)S(1)}, f32[104,128]{1,0:T(8,128)S(1)}, u32[]{:S(2)}, u32[]{:S(2)}) %collective-permute-start.58) | collective-permute-done | bytes 53280 | tf_op jit(solution)/shard_map/ppermute | solution.py:385
  173.5 5.4 %collective-permute-start.60 = (f32[104,128]{1,0:T(8,128)S(1)}, f32[104,128]{1,0:T(8,128)S(1)}, u32[]{:S(2)}, u32[]{:S(2)}) collective-permute-start(f32[104,128]{1,0:T(8,128)S(1)} %get-tuple-element.649), channel_id=1, source_target_pairs={{0,5},{4,0},{1,4},{5,1},{2,7},{6,2},{3,6},{7,3},{8,13},{12,8},{9,1... | collective-permute-start | bytes 159752 | tf_op jit(solution)/shard_map/ppermute | solution.py:385
  178.9 3.3 %collective-permute-done.60.refs_5_ = f32[104,128]{1,0:T(8,128)S(1)} collective-permute-done((f32[104,128]{1,0:T(8,128)S(1)}, f32[104,128]{1,0:T(8,128)S(1)}, u32[]{:S(2)}, u32[]{:S(2)}) %collective-permute-start.60) | collective-permute-done | bytes 53280 | tf_op jit(solution)/shard_map/ppermute | solution.py:385
  184.4 4.6 %collective-permute-start.62 = (f32[104,128]{1,0:T(8,128)S(1)}, f32[104,128]{1,0:T(8,128)S(1)}, u32[]{:S(2)}, u32[]{:S(2)}) collective-permute-start(f32[104,128]{1,0:T(8,128)S(1)} %get-tuple-element.659), channel_id=1, source_target_pairs={{0,5},{4,0},{1,4},{5,1},{2,7},{6,2},{3,6},{7,3},{8,12},{12,8},{9,1... | collective-permute-start | bytes 159752 | tf_op jit(solution)/shard_map/ppermute | solution.py:385
  189.0 3.3 %collective-permute-done.62.refs_5_ = f32[104,128]{1,0:T(8,128)S(1)} collective-permute-done((f32[104,128]{1,0:T(8,128)S(1)}, f32[104,128]{1,0:T(8,128)S(1)}, u32[]{:S(2)}, u32[]{:S(2)}) %collective-permute-start.62) | collective-permute-done | bytes 53280 | tf_op jit(solution)/shard_map/ppermute | solution.py:385
  (188 shorter events, 84.6 us)
Async XLA Ops:
  4.4 5.5 %collective-permute-start = (f32[104,128]{1,0:T(8,128)S(1)}, f32[104,128]{1,0:T(8,128)S(1)}, u32[]{:S(2)}, u32[]{:S(2)}) collective-permute-start(f32[104,128]{1,0:T(8,128)S(1)} %get-tuple-element.345), channel_id=1, source_target_pairs={{0,4},{4,1},{1,5},{5,0},{2,6},{6,3},{3,7},{7,2},{8,12},{12,8},{9,1... | collective-permute-start | bytes 159752 | tf_op jit(solution)/shard_map/ppermute | solution.py:385
  13.4 6.1 %collective-permute-start.2 = (f32[104,128]{1,0:T(8,128)S(1)}, f32[104,128]{1,0:T(8,128)S(1)}, u32[]{:S(2)}, u32[]{:S(2)}) collective-permute-start(f32[104,128]{1,0:T(8,128)S(1)} %get-tuple-element.355), channel_id=1, source_target_pairs={{0,4},{4,1},{1,5},{5,0},{2,6},{6,3},{3,7},{7,2},{8,12},{12,9},{9,1... | collective-permute-start | bytes 159752 | tf_op jit(solution)/shard_map/ppermute | solution.py:385
  22.9 5.1 %collective-permute-start.4 = (f32[104,128]{1,0:T(8,128)S(1)}, f32[104,128]{1,0:T(8,128)S(1)}, u32[]{:S(2)}, u32[]{:S(2)}) collective-permute-start(f32[104,128]{1,0:T(8,128)S(1)} %get-tuple-element.365), channel_id=1, source_target_pairs={{0,4},{4,1},{1,5},{5,0},{2,6},{6,3},{3,7},{7,2},{8,12},{12,9},{9,1... | collective-permute-start | bytes 159752 | tf_op jit(solution)/shard_map/ppermute | solution.py:385
  30.7 6.7 %collective-permute-start.7 = (f32[104,128]{1,0:T(8,128)S(1)}, f32[104,128]{1,0:T(8,128)S(1)}, u32[]{:S(2)}, u32[]{:S(2)}) collective-permute-start(f32[104,128]{1,0:T(8,128)S(1)} %get-tuple-element.382), channel_id=1, source_target_pairs={{0,4},{4,1},{1,5},{5,0},{2,6},{6,3},{3,7},{7,2},{8,12},{12,9},{9,1... | collective-permute-start | bytes 159752 | tf_op jit(solution)/shard_map/ppermute | solution.py:385
  35.6 4.9 %collective-permute-start.10 = (f32[2,104,128]{2,1,0:T(8,128)S(1)}, f32[2,104,128]{2,1,0:T(8,128)S(1)}, u32[]{:S(2)}, u32[]{:S(2)}) collective-permute-start(f32[2,104,128]{2,1,0:T(8,128)S(1)} %get-tuple-element.392), channel_id=1, source_target_pairs={{1,2},{5,6},{9,10},{13,14},{17,18},{20,21},{22,23},{25,26},{2,1},{... | collective-permute-start | bytes 319496 | tf_op jit(solution)/shard_map/ppermute | solution.py:405
  40.7 6.9 %collective-permute-start.11 = (f32[104,128]{1,0:T(8,128)S(1)}, f32[104,128]{1,0:T(8,128)S(1)}, u32[]{:S(2)}, u32[]{:S(2)}) collective-permute-start(f32[104,128]{1,0:T(8,128)S(1)} %get-tuple-element.402), channel_id=1, source_target_pairs={{0,4},{4,0},{1,5},{5,1},{2,6},{6,2},{3,7},{7,3},{8,12},{12,9},{9,1... | collective-permute-start | bytes 159752 | tf_op jit(solution)/shard_map/ppermute | solution.py:385
  49.8 7.0 %collective-permute-start.15 = (f32[104,128]{1,0:T(8,128)S(1)}, f32[104,128]{1,0:T(8,128)S(1)}, u32[]{:S(2)}, u32[]{:S(2)}) collective-permute-start(f32[104,128]{1,0:T(8,128)S(1)} %get-tuple-element.422), channel_id=1, source_target_pairs={{0,4},{4,0},{1,5},{5,1},{2,6},{6,2},{3,7},{7,3},{8,12},{12,8},{9,1... | collective-permute-start | bytes 159752 | tf_op jit(solution)/shard_map/ppermute | solution.py:385
  54.7 4.5 %collective-permute-start.18 = (f32[2,104,128]{2,1,0:T(8,128)S(1)}, f32[2,104,128]{2,1,0:T(8,128)S(1)}, u32[]{:S(2)}, u32[]{:S(2)}) collective-permute-start(f32[2,104,128]{2,1,0:T(8,128)S(1)} %get-tuple-element.432), channel_id=1, source_target_pairs={{1,2},{5,6},{9,10},{13,14},{17,18},{20,21},{22,23},{25,26},{29,30}... | collective-permute-start | bytes 319496 | tf_op jit(solution)/shard_map/ppermute | solution.py:405
  59.4 7.0 %collective-permute-start.19 = (f32[104,128]{1,0:T(8,128)S(1)}, f32[104,128]{1,0:T(8,128)S(1)}, u32[]{:S(2)}, u32[]{:S(2)}) collective-permute-start(f32[104,128]{1,0:T(8,128)S(1)} %get-tuple-element.442), channel_id=1, source_target_pairs={{0,4},{4,0},{1,5},{5,1},{2,6},{6,2},{3,7},{7,3},{8,13},{12,8},{9,1... | collective-permute-start | bytes 159752 | tf_op jit(solution)/shard_map/ppermute | solution.py:385
  67.7 9.8 %collective-permute-start.23 = (f32[104,128]{1,0:T(8,128)S(1)}, f32[104,128]{1,0:T(8,128)S(1)}, u32[]{:S(2)}, u32[]{:S(2)}) collective-permute-start(f32[104,128]{1,0:T(8,128)S(1)} %get-tuple-element.462), channel_id=1, source_target_pairs={{0,5},{4,0},{1,4},{5,1},{2,7},{6,2},{3,6},{7,3},{8,13},{12,8},{9,1... | collective-permute-start | bytes 159752 | tf_op jit(solution)/shard_map/ppermute | solution.py:385
  74.1 4.9 %collective-permute-start.26 = (f32[2,104,128]{2,1,0:T(8,128)S(1)}, f32[2,104,128]{2,1,0:T(8,128)S(1)}, u32[]{:S(2)}, u32[]{:S(2)}) collective-permute-start(f32[2,104,128]{2,1,0:T(8,128)S(1)} %get-tuple-element.472), channel_id=1, source_target_pairs={{5,6},{8,9},{10,11},{13,14},{17,18},{20,21},{22,23},{24,25},{26,27... | collective-permute-start | bytes 319496 | tf_op jit(solution)/shard_map/ppermute | solution.py:405
  80.7 9.0 %collective-permute-start.27 = (f32[104,128]{1,0:T(8,128)S(1)}, f32[104,128]{1,0:T(8,128)S(1)}, u32[]{:S(2)}, u32[]{:S(2)}) collective-permute-start(f32[104,128]{1,0:T(8,128)S(1)} %get-tuple-element.482), channel_id=1, source_target_pairs={{0,4},{4,0},{1,5},{5,1},{2,6},{6,2},{3,7},{7,3},{8,13},{12,8},{9,1... | collective-permute-start | bytes 159752 | tf_op jit(solution)/shard_map/ppermute | solution.py:385
  92.9 8.2 %collective-permute-start.31 = (f32[104,128]{1,0:T(8,128)S(1)}, f32[104,128]{1,0:T(8,128)S(1)}, u32[]{:S(2)}, u32[]{:S(2)}) collective-permute-start(f32[104,128]{1,0:T(8,128)S(1)} %get-tuple-element.502), channel_id=1, source_target_pairs={{0,4},{4,0},{1,5},{5,1},{2,6},{6,2},{3,7},{7,3},{8,12},{12,8},{9,1... | collective-permute-start | bytes 159752 | tf_op jit(solution)/shard_map/ppermute | solution.py:385
  98.5 5.3 %collective-permute-start.34 = (f32[2,104,128]{2,1,0:T(8,128)S(1)}, f32[2,104,128]{2,1,0:T(8,128)S(1)}, u32[]{:S(2)}, u32[]{:S(2)}) collective-permute-start(f32[2,104,128]{2,1,0:T(8,128)S(1)} %get-tuple-element.512), channel_id=1, source_target_pairs={{1,2},{5,6},{8,9},{10,11},{13,14},{17,18},{20,21},{22,23},{25,26},... | collective-permute-start | bytes 319496 | tf_op jit(solution)/shard_map/ppermute | solution.py:405
  104.9 6.7 %collective-permute-start.35 = (f32[104,128]{1,0:T(8,128)S(1)}, f32[104,128]{1,0:T(8,128)S(1)}, u32[]{:S(2)}, u32[]{:S(2)}) collective-permute-start(f32[104,128]{1,0:T(8,128)S(1)} %get-tuple-element.522), channel_id=1, source_target_pairs={{0,4},{4,0},{1,5},{5,1},{2,6},{6,2},{3,7},{7,3},{8,12},{12,9},{9,1... | collective-permute-start | bytes 159752 | tf_op jit(solution)/shard_map/ppermute | solution.py:385
  116.1 5.2 %collective-permute-start.39 = (f32[104,128]{1,0:T(8,128)S(1)}, f32[104,128]{1,0:T(8,128)S(1)}, u32[]{:S(2)}, u32[]{:S(2)}) collective-permute-start(f32[104,128]{1,0:T(8,128)S(1)} %get-tuple-element.542), channel_id=1, source_target_pairs={{0,4},{4,1},{1,5},{5,0},{2,6},{6,3},{3,7},{7,2},{8,12},{12,9},{9,1... | collective-permute-start | bytes 159752 | tf_op jit(solution)/shard_map/ppermute | solution.py:385
  119.1 4.9 %collective-permute-start.42 = (f32[2,104,128]{2,1,0:T(8,128)S(1)}, f32[2,104,128]{2,1,0:T(8,128)S(1)}, u32[]{:S(2)}, u32[]{:S(2)}) collective-permute-start(f32[2,104,128]{2,1,0:T(8,128)S(1)} %get-tuple-element.552), channel_id=1, source_target_pairs={{1,2},{4,5},{6,7},{8,9},{10,11},{13,14},{17,18},{20,21},{22,23},{2... | collective-permute-start | bytes 319496 | tf_op jit(solution)/shard_map/ppermute | solution.py:405
  124.3 7.5 %collective-permute-start.43 = (f32[104,128]{1,0:T(8,128)S(1)}, f32[104,128]{1,0:T(8,128)S(1)}, u32[]{:S(2)}, u32[]{:S(2)}) collective-permute-start(f32[104,128]{1,0:T(8,128)S(1)} %get-tuple-element.562), channel_id=1, source_target_pairs={{0,4},{4,0},{1,5},{5,1},{2,6},{6,2},{3,7},{7,3},{8,12},{12,9},{9,1... | collective-permute-start | bytes 159752 | tf_op jit(solution)/shard_map/ppermute | solution.py:385
  133.1 7.6 %collective-permute-start.47 = (f32[104,128]{1,0:T(8,128)S(1)}, f32[104,128]{1,0:T(8,128)S(1)}, u32[]{:S(2)}, u32[]{:S(2)}) collective-permute-start(f32[104,128]{1,0:T(8,128)S(1)} %get-tuple-element.582), channel_id=1, source_target_pairs={{0,4},{4,0},{1,5},{5,1},{2,6},{6,2},{3,7},{7,3},{8,12},{12,8},{9,1... | collective-permute-start | bytes 159752 | tf_op jit(solution)/shard_map/ppermute | solution.py:385
  141.9 7.9 %collective-permute-start.51 = (f32[104,128]{1,0:T(8,128)S(1)}, f32[104,128]{1,0:T(8,128)S(1)}, u32[]{:S(2)}, u32[]{:S(2)}) collective-permute-start(f32[104,128]{1,0:T(8,128)S(1)} %get-tuple-element.602), channel_id=1, source_target_pairs={{0,4},{4,0},{1,5},{5,1},{2,6},{6,2},{3,7},{7,3},{8,13},{12,8},{9,1... | collective-permute-start | bytes 159752 | tf_op jit(solution)/shard_map/ppermute | solution.py:385
  151.1 9.2 %collective-permute-start.55 = (f32[104,128]{1,0:T(8,128)S(1)}, f32[104,128]{1,0:T(8,128)S(1)}, u32[]{:S(2)}, u32[]{:S(2)}) collective-permute-start(f32[104,128]{1,0:T(8,128)S(1)} %get-tuple-element.622), channel_id=1, source_target_pairs={{0,5},{4,0},{1,4},{5,1},{2,7},{6,2},{3,6},{7,3},{8,13},{12,8},{9,1... | collective-permute-start | bytes 159752 | tf_op jit(solution)/shard_map/ppermute | solution.py:385
  162.5 8.8 %collective-permute-start.58 = (f32[104,128]{1,0:T(8,128)S(1)}, f32[104,128]{1,0:T(8,128)S(1)}, u32[]{:S(2)}, u32[]{:S(2)}) collective-permute-start(f32[104,128]{1,0:T(8,128)S(1)} %get-tuple-element.639), channel_id=1, source_target_pairs={{0,5},{4,0},{1,4},{5,1},{2,7},{6,2},{3,6},{7,3},{8,13},{12,8},{9,1... | collective-permute-start | bytes 159752 | tf_op jit(solution)/shard_map/ppermute | solution.py:385
  173.5 8.7 %collective-permute-start.60 = (f32[104,128]{1,0:T(8,128)S(1)}, f32[104,128]{1,0:T(8,128)S(1)}, u32[]{:S(2)}, u32[]{:S(2)}) collective-permute-start(f32[104,128]{1,0:T(8,128)S(1)} %get-tuple-element.649), channel_id=1, source_target_pairs={{0,5},{4,0},{1,4},{5,1},{2,7},{6,2},{3,6},{7,3},{8,13},{12,8},{9,1... | collective-permute-start | bytes 159752 | tf_op jit(solution)/shard_map/ppermute | solution.py:385
  184.4 7.9 %collective-permute-start.62 = (f32[104,128]{1,0:T(8,128)S(1)}, f32[104,128]{1,0:T(8,128)S(1)}, u32[]{:S(2)}, u32[]{:S(2)}) collective-permute-start(f32[104,128]{1,0:T(8,128)S(1)} %get-tuple-element.659), channel_id=1, source_target_pairs={{0,5},{4,0},{1,4},{5,1},{2,7},{6,2},{3,6},{7,3},{8,12},{12,8},{9,1... | collective-permute-start | bytes 159752 | tf_op jit(solution)/shard_map/ppermute | solution.py:385
  (39 other events, 81.9 us)
where the time goes:
time: 195 us; the launch traced here: 194 us
  starting transfers between devices  127 us (65%)
  waiting for transfers between devices  33 us (17%)
  Pallas kernels  32.2 us (17%)
    ppermute x37, starting transfers between devices, per_device(): incoming = lax.ppermute(value, ('sweep', 'span'), pairs)  103 us
    ppermute x37, waiting for transfers between devices, per_device(): incoming = lax.ppermute(value, ('sweep', 'span'), pairs)  32.2 us
    ppermute x26, starting transfers between devices, per_device(): lax.ppermute(cross[0], ('sweep', 'span'), closed(pairs, range(count * par...  23.7 us
    pallas_call x78, Pallas kernels, call(): pl.pallas_call(body, out_shape=tuple((held(shape) for shape in [*(a.shape...  17.6 us
    pallas_call x4, Pallas kernels, later_call(): pl.pallas_call(functools.partial(later_kernel, face, slot), out_shape=hel...  11.5 us
  transfers between devices with their start and end apart: 63, of which 28 were waited for; matrix products, arithmetic and copies ran while one was open for 0% of the time, Pallas kernels for 11%

commit v1 on v0

--- a/solution.py
+++ b/solution.py
@@ -226,24 +226,19 @@
                 cross[entry] = latest[vector]
 
 
-def side_kernel(came, plan, columns_and_inputs, kept, values, spare):
-    left_cols, right_cols, *arrived = columns_and_inputs
-    blocks, base, latest = kept
+def side_kernel(came, columns_and_inputs, kept, values, spare):
+    left_cols, right_cols, arrived = columns_and_inputs
+    blocks, base = kept
     place = lax.axis_index("sweep")
-    if values:
-        fill(values[0], latest, plan, place)
-    if arrived:
-        pairs = pick(numbers(came, -1), place)
-        for entry in range(arrived[0].shape[0]):
-            chosen = numbers(came, entry)
-            if any(one >= 0 for one in chosen):
-                vector = pick(chosen, place)
-
-                @pl.when(vector >= 0)
-                def _():
-                    take_lateral(
-                        base, vector, blocks, left_cols, right_cols, arrived[0][entry], spare, pairs
-                    )
+    pairs = pick(numbers(came, -1), place)
+    for entry in range(arrived.shape[0]):
+        chosen = numbers(came, entry)
+        if any(one >= 0 for one in chosen):
+            vector = pick(chosen, place)
+
+            @pl.when(vector >= 0)
+            def _():
+                take_lateral(base, vector, blocks, left_cols, right_cols, arrived[entry], spare, pairs)
 
 
 def turn_kernel(tick, vectors, columns_and_inputs, kept, values, spare):
@@ -361,13 +356,12 @@
         tasks = tasks_at(tick)
         plan = sent[tick]
         turning = any(turns(one) for one in tasks)
-        at_once = any(plan) and tick & 1 == 1
         blocks, base, latest, out, value, *cross = call(
             functools.partial(task_kernel, tick, tasks, plan),
             "task",
             (*columns, source, incoming, arrived if turning else blank),
             (blocks, base, latest, out),
-            ((rows, lanes), *([(1, rows, lanes)] if at_once else [])),
+            ((rows, lanes), *([(1 if tick & 1 else 2, rows, lanes)] if any(plan) else [])),
             (rows, lanes),
         )
 
@@ -384,17 +378,15 @@
             pairs += [(device(s, x), device(s, y)) for s in alone for a, b in even_pairs for x, y in ((a, b), (b, a))]
             incoming = lax.ppermute(value, ("sweep", "span"), pairs)
         came = [None if not tick or urgent[tick - 1][s] else sent[tick - 1][s] for s in range(count)]
-        later = any(plan) and not at_once
-        if any(came) or later:
-            blocks, base, latest, *made = call(
-                functools.partial(side_kernel, came, plan),
+        if any(came):
+            blocks, base = call(
+                functools.partial(side_kernel, came),
                 "side",
-                (columns[2], columns[3], *([arrived] if any(came) else [])),
-                (blocks, base, latest),
-                ((2, rows, lanes),) if later else (),
+                (columns[2], columns[3], arrived),
+                (blocks, base),
+                (),
                 (rows, lanes),
             )
-            cross += made
         if any(plan):
             pairs = [
                 (device(s, a), device(s, b))

time: 195 us -> 196 us (level)
    pallas_call x78 -> x76, Pallas kernels: 17.6 us -> 18.2 us  [call(): pl.pallas_call(body, out_shape=tuple((held(shape) for shape in [*(a.shape...]
  transfers between devices with their start and end apart: 63 -> 63, of which waited for: 28 -> 28; matrix products, arithmetic and copies ran while one was open for 0% -> 0% of each run, Pallas kernels for 11% -> 12%
where the time goes in v1:
time: 196 us; the launch traced here: 195 us
  starting transfers between devices  127 us (65%)
  Pallas kernels  32.7 us (17%)
  waiting for transfers between devices  32.6 us (17%)
    ppermute x37, starting transfers between devices, per_device(): incoming = lax.ppermute(value, ('sweep', 'span'), pairs)  103 us
    ppermute x37, waiting for transfers between devices, per_device(): incoming = lax.ppermute(value, ('sweep', 'span'), pairs)  31.9 us
    ppermute x26, starting transfers between devices, per_device(): lax.ppermute(cross[0], ('sweep', 'span'), closed(pairs, range(count * par...  23.6 us
    pallas_call x76, Pallas kernels, call(): pl.pallas_call(body, out_shape=tuple((held(shape) for shape in [*(a.shape...  18.2 us
    pallas_call x4, Pallas kernels, later_call(): pl.pallas_call(functools.partial(later_kernel, face, slot), out_shape=hel...  11.5 us
  transfers between devices with their start and end apart: 63, of which 28 were waited for; matrix products, arithmetic and copies ran while one was open for 0% of the time, Pallas kernels for 12%

profile of v1, /device:TPU:0, one launch (start us, length us, event | category | flops | bytes accessed | tf_op | source)
XLA Modules:
  0.0 194.8 jit_solution(15112493474055382363)
XLA Ops:
  0.9 3.0 %first.1 = (f32[5,100,104,128]{3,2,1,0:T(8,128)S(1)}, f32[4,104,128]{2,1,0:T(8,128)S(1)}, f32[4,104,128]{2,1,0:T(8,128)S(1)}, f32[104,128]{1,0:T(8,128)S(1)}, s3...) custom-call(bf16[100,100,128]{2,1,0:T(8,128)(2,1)} %bitcast.11, ...), custom_call_target="tpu_custom_call" | custom-call | tf_op jit(solution)/shard_map/first/pallas_call | solution.py:295
  10.1 2.9 %later.5.refs_7_ = f32[5,100,104,128]{3,2,1,0:T(8,128)S(1)} custom-call(bf16[1,1,3,100,100,128]{5,4,3,2,1,0:T(8,128)(2,1)} %block.7, f32[5,100,104,128]{3,2,1,0:T(8,128)S(1)} %get-tuple-element.319.blocks_in), custom_call_target="tpu_custom_call", output_to_operand_aliasing={{}: (1, {})} | custom-call | tf_op jit(solution)/shard_map/later/pallas_call | solution.py:310
  13.4 3.2 %collective-permute-start.2 = (f32[104,128]{1,0:T(8,128)S(1)}, f32[104,128]{1,0:T(8,128)S(1)}, u32[]{:S(2)}, u32[]{:S(2)}) collective-permute-start(f32[104,128]{1,0:T(8,128)S(1)} %get-tuple-element.323), channel_id=1, source_target_pairs={{0,4},{4,1},{1,5},{5,0},{2,6},{6,3},{3,7},{7,2},{8,12},{12,9},{9,1... | collective-permute-start | bytes 159752 | tf_op jit(solution)/shard_map/ppermute | solution.py:379
  19.6 2.9 %later.7.refs_7_ = f32[5,100,104,128]{3,2,1,0:T(8,128)S(1)} custom-call(bf16[1,1,3,100,100,128]{5,4,3,2,1,0:T(8,128)(2,1)} %block.7, f32[5,100,104,128]{3,2,1,0:T(8,128)S(1)} %get-tuple-element.329.blocks_in), custom_call_target="tpu_custom_call", output_to_operand_aliasing={{}: (1, {})} | custom-call | tf_op jit(solution)/shard_map/later/pallas_call | solution.py:310
  22.9 3.2 %collective-permute-start.4 = (f32[104,128]{1,0:T(8,128)S(1)}, f32[104,128]{1,0:T(8,128)S(1)}, u32[]{:S(2)}, u32[]{:S(2)}) collective-permute-start(f32[104,128]{1,0:T(8,128)S(1)} %get-tuple-element.333), channel_id=1, source_target_pairs={{0,4},{4,1},{1,5},{5,0},{2,6},{6,3},{3,7},{7,2},{8,12},{12,9},{9,1... | collective-permute-start | bytes 159752 | tf_op jit(solution)/shard_map/ppermute | solution.py:379
  30.8 5.0 %collective-permute-start.7 = (f32[104,128]{1,0:T(8,128)S(1)}, f32[104,128]{1,0:T(8,128)S(1)}, u32[]{:S(2)}, u32[]{:S(2)}) collective-permute-start(f32[104,128]{1,0:T(8,128)S(1)} %get-tuple-element.346), channel_id=1, source_target_pairs={{0,4},{4,1},{1,5},{5,0},{2,6},{6,3},{3,7},{7,2},{8,12},{12,9},{9,1... | collective-permute-start | bytes 159752 | tf_op jit(solution)/shard_map/ppermute | solution.py:379
  40.9 4.9 %collective-permute-start.11 = (f32[104,128]{1,0:T(8,128)S(1)}, f32[104,128]{1,0:T(8,128)S(1)}, u32[]{:S(2)}, u32[]{:S(2)}) collective-permute-start(f32[104,128]{1,0:T(8,128)S(1)} %get-tuple-element.362), channel_id=1, source_target_pairs={{0,4},{4,0},{1,5},{5,1},{2,6},{6,2},{3,7},{7,3},{8,12},{12,9},{9,1... | collective-permute-start | bytes 159752 | tf_op jit(solution)/shard_map/ppermute | solution.py:379
  50.0 5.0 %collective-permute-start.15 = (f32[104,128]{1,0:T(8,128)S(1)}, f32[104,128]{1,0:T(8,128)S(1)}, u32[]{:S(2)}, u32[]{:S(2)}) collective-permute-start(f32[104,128]{1,0:T(8,128)S(1)} %get-tuple-element.380), channel_id=1, source_target_pairs={{0,4},{4,0},{1,5},{5,1},{2,6},{6,2},{3,7},{7,3},{8,12},{12,8},{9,1... | collective-permute-start | bytes 159752 | tf_op jit(solution)/shard_map/ppermute | solution.py:379
  59.7 4.7 %collective-permute-start.19 = (f32[104,128]{1,0:T(8,128)S(1)}, f32[104,128]{1,0:T(8,128)S(1)}, u32[]{:S(2)}, u32[]{:S(2)}) collective-permute-start(f32[104,128]{1,0:T(8,128)S(1)} %get-tuple-element.398), channel_id=1, source_target_pairs={{0,4},{4,0},{1,5},{5,1},{2,6},{6,2},{3,7},{7,3},{8,13},{12,8},{9,1... | collective-permute-start | bytes 159752 | tf_op jit(solution)/shard_map/ppermute | solution.py:379
  67.8 6.6 %collective-permute-start.23 = (f32[104,128]{1,0:T(8,128)S(1)}, f32[104,128]{1,0:T(8,128)S(1)}, u32[]{:S(2)}, u32[]{:S(2)}) collective-permute-start(f32[104,128]{1,0:T(8,128)S(1)} %get-tuple-element.416), channel_id=1, source_target_pairs={{0,5},{4,0},{1,4},{5,1},{2,7},{6,2},{3,6},{7,3},{8,13},{12,8},{9,1... | collective-permute-start | bytes 159752 | tf_op jit(solution)/shard_map/ppermute | solution.py:379
  80.9 6.6 %collective-permute-start.27 = (f32[104,128]{1,0:T(8,128)S(1)}, f32[104,128]{1,0:T(8,128)S(1)}, u32[]{:S(2)}, u32[]{:S(2)}) collective-permute-start(f32[104,128]{1,0:T(8,128)S(1)} %get-tuple-element.434), channel_id=1, source_target_pairs={{0,4},{4,0},{1,5},{5,1},{2,6},{6,2},{3,7},{7,3},{8,13},{12,8},{9,1... | collective-permute-start | bytes 159752 | tf_op jit(solution)/shard_map/ppermute | solution.py:379
  93.1 5.6 %collective-permute-start.31 = (f32[104,128]{1,0:T(8,128)S(1)}, f32[104,128]{1,0:T(8,128)S(1)}, u32[]{:S(2)}, u32[]{:S(2)}) collective-permute-start(f32[104,128]{1,0:T(8,128)S(1)} %get-tuple-element.452), channel_id=1, source_target_pairs={{0,4},{4,0},{1,5},{5,1},{2,6},{6,2},{3,7},{7,3},{8,12},{12,8},{9,1... | collective-permute-start | bytes 159752 | tf_op jit(solution)/shard_map/ppermute | solution.py:379
  105.1 4.6 %collective-permute-start.35 = (f32[104,128]{1,0:T(8,128)S(1)}, f32[104,128]{1,0:T(8,128)S(1)}, u32[]{:S(2)}, u32[]{:S(2)}) collective-permute-start(f32[104,128]{1,0:T(8,128)S(1)} %get-tuple-element.470), channel_id=1, source_target_pairs={{0,4},{4,0},{1,5},{5,1},{2,6},{6,2},{3,7},{7,3},{8,12},{12,9},{9,1... | collective-permute-start | bytes 159752 | tf_op jit(solution)/shard_map/ppermute | solution.py:379
  116.2 3.1 %collective-permute-start.39 = (f32[104,128]{1,0:T(8,128)S(1)}, f32[104,128]{1,0:T(8,128)S(1)}, u32[]{:S(2)}, u32[]{:S(2)}) collective-permute-start(f32[104,128]{1,0:T(8,128)S(1)} %get-tuple-element.488), channel_id=1, source_target_pairs={{0,4},{4,1},{1,5},{5,0},{2,6},{6,3},{3,7},{7,2},{8,12},{12,9},{9,1... | collective-permute-start | bytes 159752 | tf_op jit(solution)/shard_map/ppermute | solution.py:379
  124.4 5.1 %collective-permute-start.43 = (f32[104,128]{1,0:T(8,128)S(1)}, f32[104,128]{1,0:T(8,128)S(1)}, u32[]{:S(2)}, u32[]{:S(2)}) collective-permute-start(f32[104,128]{1,0:T(8,128)S(1)} %get-tuple-element.506), channel_id=1, source_target_pairs={{0,4},{4,0},{1,5},{5,1},{2,6},{6,2},{3,7},{7,3},{8,12},{12,9},{9,1... | collective-permute-start | bytes 159752 | tf_op jit(solution)/shard_map/ppermute | solution.py:379
  133.4 5.5 %collective-permute-start.47 = (f32[104,128]{1,0:T(8,128)S(1)}, f32[104,128]{1,0:T(8,128)S(1)}, u32[]{:S(2)}, u32[]{:S(2)}) collective-permute-start(f32[104,128]{1,0:T(8,128)S(1)} %get-tuple-element.524), channel_id=1, source_target_pairs={{0,4},{4,0},{1,5},{5,1},{2,6},{6,2},{3,7},{7,3},{8,12},{12,8},{9,1... | collective-permute-start | bytes 159752 | tf_op jit(solution)/shard_map/ppermute | solution.py:379
  142.2 5.8 %collective-permute-start.51 = (f32[104,128]{1,0:T(8,128)S(1)}, f32[104,128]{1,0:T(8,128)S(1)}, u32[]{:S(2)}, u32[]{:S(2)}) collective-permute-start(f32[104,128]{1,0:T(8,128)S(1)} %get-tuple-element.542), channel_id=1, source_target_pairs={{0,4},{4,0},{1,5},{5,1},{2,6},{6,2},{3,7},{7,3},{8,13},{12,8},{9,1... | collective-permute-start | bytes 159752 | tf_op jit(solution)/shard_map/ppermute | solution.py:379
  151.4 6.2 %collective-permute-start.55 = (f32[104,128]{1,0:T(8,128)S(1)}, f32[104,128]{1,0:T(8,128)S(1)}, u32[]{:S(2)}, u32[]{:S(2)}) collective-permute-start(f32[104,128]{1,0:T(8,128)S(1)} %get-tuple-element.560), channel_id=1, source_target_pairs={{0,5},{4,0},{1,4},{5,1},{2,7},{6,2},{3,6},{7,3},{8,13},{12,8},{9,1... | collective-permute-start | bytes 159752 | tf_op jit(solution)/shard_map/ppermute | solution.py:379
  162.8 5.9 %collective-permute-start.58 = (f32[104,128]{1,0:T(8,128)S(1)}, f32[104,128]{1,0:T(8,128)S(1)}, u32[]{:S(2)}, u32[]{:S(2)}) collective-permute-start(f32[104,128]{1,0:T(8,128)S(1)} %get-tuple-element.575), channel_id=1, source_target_pairs={{0,5},{4,0},{1,4},{5,1},{2,7},{6,2},{3,6},{7,3},{8,13},{12,8},{9,1... | collective-permute-start | bytes 159752 | tf_op jit(solution)/shard_map/ppermute | solution.py:379
  168.7 3.1 %collective-permute-done.58.refs_5_ = f32[104,128]{1,0:T(8,128)S(1)} collective-permute-done((f32[104,128]{1,0:T(8,128)S(1)}, f32[104,128]{1,0:T(8,128)S(1)}, u32[]{:S(2)}, u32[]{:S(2)}) %collective-permute-start.58) | collective-permute-done | bytes 53280 | tf_op jit(solution)/shard_map/ppermute | solution.py:379
  174.0 5.2 %collective-permute-start.60 = (f32[104,128]{1,0:T(8,128)S(1)}, f32[104,128]{1,0:T(8,128)S(1)}, u32[]{:S(2)}, u32[]{:S(2)}) collective-permute-start(f32[104,128]{1,0:T(8,128)S(1)} %get-tuple-element.585), channel_id=1, source_target_pairs={{0,5},{4,0},{1,4},{5,1},{2,7},{6,2},{3,6},{7,3},{8,13},{12,8},{9,1... | collective-permute-start | bytes 159752 | tf_op jit(solution)/shard_map/ppermute | solution.py:379
  179.2 3.3 %collective-permute-done.60.refs_5_ = f32[104,128]{1,0:T(8,128)S(1)} collective-permute-done((f32[104,128]{1,0:T(8,128)S(1)}, f32[104,128]{1,0:T(8,128)S(1)}, u32[]{:S(2)}, u32[]{:S(2)}) %collective-permute-start.60) | collective-permute-done | bytes 53280 | tf_op jit(solution)/shard_map/ppermute | solution.py:379
  184.7 4.6 %collective-permute-start.62 = (f32[104,128]{1,0:T(8,128)S(1)}, f32[104,128]{1,0:T(8,128)S(1)}, u32[]{:S(2)}, u32[]{:S(2)}) collective-permute-start(f32[104,128]{1,0:T(8,128)S(1)} %get-tuple-element.595), channel_id=1, source_target_pairs={{0,5},{4,0},{1,4},{5,1},{2,7},{6,2},{3,6},{7,3},{8,12},{12,8},{9,1... | collective-permute-start | bytes 159752 | tf_op jit(solution)/shard_map/ppermute | solution.py:379
  189.3 3.3 %collective-permute-done.62.refs_5_ = f32[104,128]{1,0:T(8,128)S(1)} collective-permute-done((f32[104,128]{1,0:T(8,128)S(1)}, f32[104,128]{1,0:T(8,128)S(1)}, u32[]{:S(2)}, u32[]{:S(2)}) %collective-permute-start.62) | collective-permute-done | bytes 53280 | tf_op jit(solution)/shard_map/ppermute | solution.py:379
  (186 shorter events, 84.5 us)
Async XLA Ops:
  4.4 5.5 %collective-permute-start = (f32[104,128]{1,0:T(8,128)S(1)}, f32[104,128]{1,0:T(8,128)S(1)}, u32[]{:S(2)}, u32[]{:S(2)}) collective-permute-start(f32[104,128]{1,0:T(8,128)S(1)} %get-tuple-element.313), channel_id=1, source_target_pairs={{0,4},{4,1},{1,5},{5,0},{2,6},{6,3},{3,7},{7,2},{8,12},{12,8},{9,1... | collective-permute-start | bytes 159752 | tf_op jit(solution)/shard_map/ppermute | solution.py:379
  13.4 6.1 %collective-permute-start.2 = (f32[104,128]{1,0:T(8,128)S(1)}, f32[104,128]{1,0:T(8,128)S(1)}, u32[]{:S(2)}, u32[]{:S(2)}) collective-permute-start(f32[104,128]{1,0:T(8,128)S(1)} %get-tuple-element.323), channel_id=1, source_target_pairs={{0,4},{4,1},{1,5},{5,0},{2,6},{6,3},{3,7},{7,2},{8,12},{12,9},{9,1... | collective-permute-start | bytes 159752 | tf_op jit(solution)/shard_map/ppermute | solution.py:379
  22.9 5.2 %collective-permute-start.4 = (f32[104,128]{1,0:T(8,128)S(1)}, f32[104,128]{1,0:T(8,128)S(1)}, u32[]{:S(2)}, u32[]{:S(2)}) collective-permute-start(f32[104,128]{1,0:T(8,128)S(1)} %get-tuple-element.333), channel_id=1, source_target_pairs={{0,4},{4,1},{1,5},{5,0},{2,6},{6,3},{3,7},{7,2},{8,12},{12,9},{9,1... | collective-permute-start | bytes 159752 | tf_op jit(solution)/shard_map/ppermute | solution.py:379
  30.8 6.8 %collective-permute-start.7 = (f32[104,128]{1,0:T(8,128)S(1)}, f32[104,128]{1,0:T(8,128)S(1)}, u32[]{:S(2)}, u32[]{:S(2)}) collective-permute-start(f32[104,128]{1,0:T(8,128)S(1)} %get-tuple-element.346), channel_id=1, source_target_pairs={{0,4},{4,1},{1,5},{5,0},{2,6},{6,3},{3,7},{7,2},{8,12},{12,9},{9,1... | collective-permute-start | bytes 159752 | tf_op jit(solution)/shard_map/ppermute | solution.py:379
  35.8 4.9 %collective-permute-start.10 = (f32[2,104,128]{2,1,0:T(8,128)S(1)}, f32[2,104,128]{2,1,0:T(8,128)S(1)}, u32[]{:S(2)}, u32[]{:S(2)}) collective-permute-start(f32[2,104,128]{2,1,0:T(8,128)S(1)} %get-tuple-element.353), channel_id=1, source_target_pairs={{1,2},{5,6},{9,10},{13,14},{17,18},{20,21},{22,23},{25,26},{2,1},{... | collective-permute-start | bytes 319496 | tf_op jit(solution)/shard_map/ppermute | solution.py:397
  40.9 7.0 %collective-permute-start.11 = (f32[104,128]{1,0:T(8,128)S(1)}, f32[104,128]{1,0:T(8,128)S(1)}, u32[]{:S(2)}, u32[]{:S(2)}) collective-permute-start(f32[104,128]{1,0:T(8,128)S(1)} %get-tuple-element.362), channel_id=1, source_target_pairs={{0,4},{4,0},{1,5},{5,1},{2,6},{6,2},{3,7},{7,3},{8,12},{12,9},{9,1... | collective-permute-start | bytes 159752 | tf_op jit(solution)/shard_map/ppermute | solution.py:379
  50.0 7.1 %collective-permute-start.15 = (f32[104,128]{1,0:T(8,128)S(1)}, f32[104,128]{1,0:T(8,128)S(1)}, u32[]{:S(2)}, u32[]{:S(2)}) collective-permute-start(f32[104,128]{1,0:T(8,128)S(1)} %get-tuple-element.380), channel_id=1, source_target_pairs={{0,4},{4,0},{1,5},{5,1},{2,6},{6,2},{3,7},{7,3},{8,12},{12,8},{9,1... | collective-permute-start | bytes 159752 | tf_op jit(solution)/shard_map/ppermute | solution.py:379
  55.0 4.5 %collective-permute-start.18 = (f32[2,104,128]{2,1,0:T(8,128)S(1)}, f32[2,104,128]{2,1,0:T(8,128)S(1)}, u32[]{:S(2)}, u32[]{:S(2)}) collective-permute-start(f32[2,104,128]{2,1,0:T(8,128)S(1)} %get-tuple-element.389), channel_id=1, source_target_pairs={{1,2},{5,6},{9,10},{13,14},{17,18},{20,21},{22,23},{25,26},{29,30}... | collective-permute-start | bytes 319496 | tf_op jit(solution)/shard_map/ppermute | solution.py:397
  59.7 6.8 %collective-permute-start.19 = (f32[104,128]{1,0:T(8,128)S(1)}, f32[104,128]{1,0:T(8,128)S(1)}, u32[]{:S(2)}, u32[]{:S(2)}) collective-permute-start(f32[104,128]{1,0:T(8,128)S(1)} %get-tuple-element.398), channel_id=1, source_target_pairs={{0,4},{4,0},{1,5},{5,1},{2,6},{6,2},{3,7},{7,3},{8,13},{12,8},{9,1... | collective-permute-start | bytes 159752 | tf_op jit(solution)/shard_map/ppermute | solution.py:379
  67.8 9.8 %collective-permute-start.23 = (f32[104,128]{1,0:T(8,128)S(1)}, f32[104,128]{1,0:T(8,128)S(1)}, u32[]{:S(2)}, u32[]{:S(2)}) collective-permute-start(f32[104,128]{1,0:T(8,128)S(1)} %get-tuple-element.416), channel_id=1, source_target_pairs={{0,5},{4,0},{1,4},{5,1},{2,7},{6,2},{3,6},{7,3},{8,13},{12,8},{9,1... | collective-permute-start | bytes 159752 | tf_op jit(solution)/shard_map/ppermute | solution.py:379
  74.4 4.8 %collective-permute-start.26 = (f32[2,104,128]{2,1,0:T(8,128)S(1)}, f32[2,104,128]{2,1,0:T(8,128)S(1)}, u32[]{:S(2)}, u32[]{:S(2)}) collective-permute-start(f32[2,104,128]{2,1,0:T(8,128)S(1)} %get-tuple-element.425), channel_id=1, source_target_pairs={{5,6},{8,9},{10,11},{13,14},{17,18},{20,21},{22,23},{24,25},{26,27... | collective-permute-start | bytes 319496 | tf_op jit(solution)/shard_map/ppermute | solution.py:397
  80.9 8.9 %collective-permute-start.27 = (f32[104,128]{1,0:T(8,128)S(1)}, f32[104,128]{1,0:T(8,128)S(1)}, u32[]{:S(2)}, u32[]{:S(2)}) collective-permute-start(f32[104,128]{1,0:T(8,128)S(1)} %get-tuple-element.434), channel_id=1, source_target_pairs={{0,4},{4,0},{1,5},{5,1},{2,6},{6,2},{3,7},{7,3},{8,13},{12,8},{9,1... | collective-permute-start | bytes 159752 | tf_op jit(solution)/shard_map/ppermute | solution.py:379
  93.1 8.2 %collective-permute-start.31 = (f32[104,128]{1,0:T(8,128)S(1)}, f32[104,128]{1,0:T(8,128)S(1)}, u32[]{:S(2)}, u32[]{:S(2)}) collective-permute-start(f32[104,128]{1,0:T(8,128)S(1)} %get-tuple-element.452), channel_id=1, source_target_pairs={{0,4},{4,0},{1,5},{5,1},{2,6},{6,2},{3,7},{7,3},{8,12},{12,8},{9,1... | collective-permute-start | bytes 159752 | tf_op jit(solution)/shard_map/ppermute | solution.py:379
  98.6 5.2 %collective-permute-start.34 = (f32[2,104,128]{2,1,0:T(8,128)S(1)}, f32[2,104,128]{2,1,0:T(8,128)S(1)}, u32[]{:S(2)}, u32[]{:S(2)}) collective-permute-start(f32[2,104,128]{2,1,0:T(8,128)S(1)} %get-tuple-element.461), channel_id=1, source_target_pairs={{1,2},{5,6},{8,9},{10,11},{13,14},{17,18},{20,21},{22,23},{25,26},... | collective-permute-start | bytes 319496 | tf_op jit(solution)/shard_map/ppermute | solution.py:397
  105.1 6.7 %collective-permute-start.35 = (f32[104,128]{1,0:T(8,128)S(1)}, f32[104,128]{1,0:T(8,128)S(1)}, u32[]{:S(2)}, u32[]{:S(2)}) collective-permute-start(f32[104,128]{1,0:T(8,128)S(1)} %get-tuple-element.470), channel_id=1, source_target_pairs={{0,4},{4,0},{1,5},{5,1},{2,6},{6,2},{3,7},{7,3},{8,12},{12,9},{9,1... | collective-permute-start | bytes 159752 | tf_op jit(solution)/shard_map/ppermute | solution.py:379
  116.2 5.3 %collective-permute-start.39 = (f32[104,128]{1,0:T(8,128)S(1)}, f32[104,128]{1,0:T(8,128)S(1)}, u32[]{:S(2)}, u32[]{:S(2)}) collective-permute-start(f32[104,128]{1,0:T(8,128)S(1)} %get-tuple-element.488), channel_id=1, source_target_pairs={{0,4},{4,1},{1,5},{5,0},{2,6},{6,3},{3,7},{7,2},{8,12},{12,9},{9,1... | collective-permute-start | bytes 159752 | tf_op jit(solution)/shard_map/ppermute | solution.py:379
  119.3 4.9 %collective-permute-start.42 = (f32[2,104,128]{2,1,0:T(8,128)S(1)}, f32[2,104,128]{2,1,0:T(8,128)S(1)}, u32[]{:S(2)}, u32[]{:S(2)}) collective-permute-start(f32[2,104,128]{2,1,0:T(8,128)S(1)} %get-tuple-element.497), channel_id=1, source_target_pairs={{1,2},{4,5},{6,7},{8,9},{10,11},{13,14},{17,18},{20,21},{22,23},{2... | collective-permute-start | bytes 319496 | tf_op jit(solution)/shard_map/ppermute | solution.py:397
  124.4 7.6 %collective-permute-start.43 = (f32[104,128]{1,0:T(8,128)S(1)}, f32[104,128]{1,0:T(8,128)S(1)}, u32[]{:S(2)}, u32[]{:S(2)}) collective-permute-start(f32[104,128]{1,0:T(8,128)S(1)} %get-tuple-element.506), channel_id=1, source_target_pairs={{0,4},{4,0},{1,5},{5,1},{2,6},{6,2},{3,7},{7,3},{8,12},{12,9},{9,1... | collective-permute-start | bytes 159752 | tf_op jit(solution)/shard_map/ppermute | solution.py:379
  133.4 7.6 %collective-permute-start.47 = (f32[104,128]{1,0:T(8,128)S(1)}, f32[104,128]{1,0:T(8,128)S(1)}, u32[]{:S(2)}, u32[]{:S(2)}) collective-permute-start(f32[104,128]{1,0:T(8,128)S(1)} %get-tuple-element.524), channel_id=1, source_target_pairs={{0,4},{4,0},{1,5},{5,1},{2,6},{6,2},{3,7},{7,3},{8,12},{12,8},{9,1... | collective-permute-start | bytes 159752 | tf_op jit(solution)/shard_map/ppermute | solution.py:379
  142.2 7.9 %collective-permute-start.51 = (f32[104,128]{1,0:T(8,128)S(1)}, f32[104,128]{1,0:T(8,128)S(1)}, u32[]{:S(2)}, u32[]{:S(2)}) collective-permute-start(f32[104,128]{1,0:T(8,128)S(1)} %get-tuple-element.542), channel_id=1, source_target_pairs={{0,4},{4,0},{1,5},{5,1},{2,6},{6,2},{3,7},{7,3},{8,13},{12,8},{9,1... | collective-permute-start | bytes 159752 | tf_op jit(solution)/shard_map/ppermute | solution.py:379
  151.4 9.2 %collective-permute-start.55 = (f32[104,128]{1,0:T(8,128)S(1)}, f32[104,128]{1,0:T(8,128)S(1)}, u32[]{:S(2)}, u32[]{:S(2)}) collective-permute-start(f32[104,128]{1,0:T(8,128)S(1)} %get-tuple-element.560), channel_id=1, source_target_pairs={{0,5},{4,0},{1,4},{5,1},{2,7},{6,2},{3,6},{7,3},{8,13},{12,8},{9,1... | collective-permute-start | bytes 159752 | tf_op jit(solution)/shard_map/ppermute | solution.py:379
  162.8 9.0 %collective-permute-start.58 = (f32[104,128]{1,0:T(8,128)S(1)}, f32[104,128]{1,0:T(8,128)S(1)}, u32[]{:S(2)}, u32[]{:S(2)}) collective-permute-start(f32[104,128]{1,0:T(8,128)S(1)} %get-tuple-element.575), channel_id=1, source_target_pairs={{0,5},{4,0},{1,4},{5,1},{2,7},{6,2},{3,6},{7,3},{8,13},{12,8},{9,1... | collective-permute-start | bytes 159752 | tf_op jit(solution)/shard_map/ppermute | solution.py:379
  174.0 8.5 %collective-permute-start.60 = (f32[104,128]{1,0:T(8,128)S(1)}, f32[104,128]{1,0:T(8,128)S(1)}, u32[]{:S(2)}, u32[]{:S(2)}) collective-permute-start(f32[104,128]{1,0:T(8,128)S(1)} %get-tuple-element.585), channel_id=1, source_target_pairs={{0,5},{4,0},{1,4},{5,1},{2,7},{6,2},{3,6},{7,3},{8,13},{12,8},{9,1... | collective-permute-start | bytes 159752 | tf_op jit(solution)/shard_map/ppermute | solution.py:379
  184.7 7.9 %collective-permute-start.62 = (f32[104,128]{1,0:T(8,128)S(1)}, f32[104,128]{1,0:T(8,128)S(1)}, u32[]{:S(2)}, u32[]{:S(2)}) collective-permute-start(f32[104,128]{1,0:T(8,128)S(1)} %get-tuple-element.595), channel_id=1, source_target_pairs={{0,5},{4,0},{1,4},{5,1},{2,7},{6,2},{3,6},{7,3},{8,12},{12,8},{9,1... | collective-permute-start | bytes 159752 | tf_op jit(solution)/shard_map/ppermute | solution.py:379
  (39 other events, 81.8 us)

commit v2 on v1

--- a/solution.py
+++ b/solution.py
@@ -36,32 +36,45 @@
     sent = [[None] * count for _ in range(ticks)]
     urgent = [[False] * count for _ in range(ticks)]
     for slab in range(count):
-        left = ([], [])
-        for half in range(3):
+        fixed, waiting, busy = [], ([], []), set()
+        for half in range(4):
             rank = count - 1 - slab if half & 1 else slab
             for vector in range(vectors):
                 made = 2 * vector + half * count + rank
                 used = 2 * vector + (half + 1) * count + count - 1 - rank
+                busy.add(made)
+                if half == 3:
+                    continue
                 if used == made + 1:
-                    sent[made][slab] = (1, (vector,))
+                    fixed.append((made, (1, (vector,))))
                     urgent[made][slab] = True
                     continue
-                left[1].append((used, made, vector))
+                waiting[1].append((used, made, vector))
                 if used == made + 3:
-                    sent[made + 1][slab] = (0, (vector,))
+                    fixed.append((made + 1, (0, (vector,))))
                 else:
-                    left[0].append((used, made, vector))
-        for tick in range(LATERAL_START, ticks, 2):
-            ready = [sorted(one for one in waiting if one[1] <= tick)[:2] for waiting in left]
-            if not any(ready):
-                continue
-            pairs = 0 if ready[0] and (not ready[1] or ready[0][0][0] <= ready[1][0][0]) else 1
-            assert tick <= ready[pairs][0][0] - 2
-            sent[tick][slab] = (pairs, tuple(one[2] for one in ready[pairs]))
-            for one in ready[pairs]:
-                left[pairs].remove(one)
-        assert not any(left)
+                    waiting[0].append((used, made, vector))
+        even = range(LATERAL_START, ticks, 2)
+        found = in_order(waiting, [tick for tick in even if tick not in busy]) or in_order(waiting, even)
+        for tick, one in (*fixed, *found):
+            sent[tick][slab] = one
     return sent, urgent
+
+
+def in_order(waiting, slots):
+    left = tuple(list(kind) for kind in waiting)
+    found = []
+    for tick in slots:
+        ready = [sorted(one for one in kind if one[1] <= tick)[:2] for kind in left]
+        if not any(ready):
+            continue
+        pairs = 0 if ready[0] and (not ready[1] or ready[0][0][0] <= ready[1][0][0]) else 1
+        if tick > ready[pairs][0][0] - 2:
+            return None
+        found.append((tick, (pairs, tuple(one[2] for one in ready[pairs]))))
+        for one in ready[pairs]:
+            left[pairs].remove(one)
+    return None if any(left) else found
 
 
 def numbers(plan, entry):
@@ -153,10 +166,11 @@
     for copy in copies:
         copy.start()
     prepare(block, blocks.at[DIAG], narrow, wide, sems)
-    vectors, size, lanes = residual.shape
+    size, vectors, lanes = residual.shape
     rows = base.shape[1]
     base[:, pl.ds(rows - SUBLANES, SUBLANES), :] = jnp.zeros((vectors, SUBLANES, lanes), jnp.float32)
-    base[:, pl.ds(0, size), :] = residual[...]
+    for vector in range(vectors):
+        base[vector, pl.ds(0, size), :] = residual[:, vector, :]
     source[...] = base[...]
     blank[...] = jnp.zeros_like(blank)
     for copy in copies:
@@ -289,7 +303,7 @@
 
 
 def first_call(block, residual, columns, rows):
-    vectors, size, lanes = residual.shape
+    size, vectors, lanes = residual.shape
     several = (vectors, rows, lanes)
     in_hbm = pl.BlockSpec(memory_space=pltpu.HBM)
     return pl.pallas_call(
@@ -339,7 +353,9 @@
     def device(slab, part):
         return slab * parts + part
 
-    blocks, base, source, blank, *columns = first_call(diag_inverse[0, 0], residual_in[0, 0], columns, rows)
+    blocks, base, source, blank, *columns = first_call(
+        diag_inverse[0, 0], jnp.transpose(residual_in[0, 0], (1, 0, 2)), columns, rows
+    )
     latest, out = pl.pallas_call(
         lambda *refs: None,
         out_shape=(held((vectors, rows, lanes)), held((vectors, size, lanes))),

time: 196 us -> 196 us (level)
    ppermute x37, waiting for transfers between devices: 31.9 us -> 33.9 us  [per_device(): incoming = lax.ppermute(value, ('sweep', 'span'), pairs)]
  transfers between devices with their start and end apart: 63 -> 63, of which waited for: 28 -> 29; matrix products, arithmetic and copies ran while one was open for 0% -> 0% of each run, Pallas kernels for 12% -> 11%
where the time goes in v2:
time: 196 us; the launch traced here: 195 us
  starting transfers between devices  126 us (64%)
  waiting for transfers between devices  34 us (17%)
  Pallas kernels  32.8 us (17%)
    ppermute x37, starting transfers between devices, per_device(): incoming = lax.ppermute(value, ('sweep', 'span'), pairs)  103 us
    ppermute x37, waiting for transfers between devices, per_device(): incoming = lax.ppermute(value, ('sweep', 'span'), pairs)  33.9 us
    ppermute x26, starting transfers between devices, per_device(): lax.ppermute(cross[0], ('sweep', 'span'), closed(pairs, range(count * par...  22.5 us
    pallas_call x76, Pallas kernels, call(): pl.pallas_call(body, out_shape=tuple((held(shape) for shape in [*(a.shape...  18.1 us
    pallas_call x4, Pallas kernels, later_call(): pl.pallas_call(functools.partial(later_kernel, face, slot), out_shape=hel...  11.5 us
  transfers between devices with their start and end apart: 63, of which 29 were waited for; matrix products, arithmetic and copies ran while one was open for 0% of the time, Pallas kernels for 11%

profile of v2, /device:TPU:0, one launch (start us, length us, event | category | flops | bytes accessed | tf_op | source)
XLA Modules:
  0.0 194.9 jit_solution(13123034523380348819)
XLA Ops:
  0.9 3.1 %first.1 = (f32[5,100,104,128]{3,2,1,0:T(8,128)S(1)}, f32[4,104,128]{2,1,0:T(8,128)S(1)}, f32[4,104,128]{2,1,0:T(8,128)S(1)}, f32[104,128]{1,0:T(8,128)S(1)}, s3...) custom-call(bf16[100,100,128]{2,1,0:T(8,128)(2,1)} %bitcast.11, ...), custom_call_target="tpu_custom_call" | custom-call | tf_op jit(solution)/shard_map/first/pallas_call | solution.py:309
  10.1 2.9 %later.5.refs_7_ = f32[5,100,104,128]{3,2,1,0:T(8,128)S(1)} custom-call(bf16[1,1,3,100,100,128]{5,4,3,2,1,0:T(8,128)(2,1)} %block.7, f32[5,100,104,128]{3,2,1,0:T(8,128)S(1)} %get-tuple-element.319.blocks_in), custom_call_target="tpu_custom_call", output_to_operand_aliasing={{}: (1, {})} | custom-call | tf_op jit(solution)/shard_map/later/pallas_call | solution.py:324
  13.4 3.2 %collective-permute-start.2 = (f32[104,128]{1,0:T(8,128)S(1)}, f32[104,128]{1,0:T(8,128)S(1)}, u32[]{:S(2)}, u32[]{:S(2)}) collective-permute-start(f32[104,128]{1,0:T(8,128)S(1)} %get-tuple-element.323), channel_id=1, source_target_pairs={{0,4},{4,1},{1,5},{5,0},{2,6},{6,3},{3,7},{7,2},{8,12},{12,9},{9,1... | collective-permute-start | bytes 159752 | tf_op jit(solution)/shard_map/ppermute | solution.py:395
  19.6 2.9 %later.7.refs_7_ = f32[5,100,104,128]{3,2,1,0:T(8,128)S(1)} custom-call(bf16[1,1,3,100,100,128]{5,4,3,2,1,0:T(8,128)(2,1)} %block.7, f32[5,100,104,128]{3,2,1,0:T(8,128)S(1)} %get-tuple-element.329.blocks_in), custom_call_target="tpu_custom_call", output_to_operand_aliasing={{}: (1, {})} | custom-call | tf_op jit(solution)/shard_map/later/pallas_call | solution.py:324
  23.0 3.3 %collective-permute-start.4 = (f32[104,128]{1,0:T(8,128)S(1)}, f32[104,128]{1,0:T(8,128)S(1)}, u32[]{:S(2)}, u32[]{:S(2)}) collective-permute-start(f32[104,128]{1,0:T(8,128)S(1)} %get-tuple-element.333), channel_id=1, source_target_pairs={{0,4},{4,1},{1,5},{5,0},{2,6},{6,3},{3,7},{7,2},{8,12},{12,9},{9,1... | collective-permute-start | bytes 159752 | tf_op jit(solution)/shard_map/ppermute | solution.py:395
  29.7 6.1 %collective-permute-start.7 = (f32[104,128]{1,0:T(8,128)S(1)}, f32[104,128]{1,0:T(8,128)S(1)}, u32[]{:S(2)}, u32[]{:S(2)}) collective-permute-start(f32[104,128]{1,0:T(8,128)S(1)} %get-tuple-element.346), channel_id=1, source_target_pairs={{0,4},{4,1},{1,5},{5,0},{2,6},{6,3},{3,7},{7,2},{8,12},{12,9},{9,1... | collective-permute-start | bytes 159752 | tf_op jit(solution)/shard_map/ppermute | solution.py:395
  38.9 6.9 %collective-permute-start.11 = (f32[104,128]{1,0:T(8,128)S(1)}, f32[104,128]{1,0:T(8,128)S(1)}, u32[]{:S(2)}, u32[]{:S(2)}) collective-permute-start(f32[104,128]{1,0:T(8,128)S(1)} %get-tuple-element.362), channel_id=1, source_target_pairs={{0,4},{4,0},{1,5},{5,1},{2,6},{6,2},{3,7},{7,3},{8,12},{12,9},{9,1... | collective-permute-start | bytes 159752 | tf_op jit(solution)/shard_map/ppermute | solution.py:395
  50.1 4.9 %collective-permute-start.15 = (f32[104,128]{1,0:T(8,128)S(1)}, f32[104,128]{1,0:T(8,128)S(1)}, u32[]{:S(2)}, u32[]{:S(2)}) collective-permute-start(f32[104,128]{1,0:T(8,128)S(1)} %get-tuple-element.380), channel_id=1, source_target_pairs={{0,4},{4,0},{1,5},{5,1},{2,6},{6,2},{3,7},{7,3},{8,12},{12,8},{9,1... | collective-permute-start | bytes 159752 | tf_op jit(solution)/shard_map/ppermute | solution.py:395
  59.8 4.7 %collective-permute-start.19 = (f32[104,128]{1,0:T(8,128)S(1)}, f32[104,128]{1,0:T(8,128)S(1)}, u32[]{:S(2)}, u32[]{:S(2)}) collective-permute-start(f32[104,128]{1,0:T(8,128)S(1)} %get-tuple-element.398), channel_id=1, source_target_pairs={{0,4},{4,0},{1,5},{5,1},{2,6},{6,2},{3,7},{7,3},{8,13},{12,8},{9,1... | collective-permute-start | bytes 159752 | tf_op jit(solution)/shard_map/ppermute | solution.py:395
  68.8 5.6 %collective-permute-start.23 = (f32[104,128]{1,0:T(8,128)S(1)}, f32[104,128]{1,0:T(8,128)S(1)}, u32[]{:S(2)}, u32[]{:S(2)}) collective-permute-start(f32[104,128]{1,0:T(8,128)S(1)} %get-tuple-element.416), channel_id=1, source_target_pairs={{0,5},{4,0},{1,4},{5,1},{2,7},{6,2},{3,6},{7,3},{8,13},{12,8},{9,1... | collective-permute-start | bytes 159752 | tf_op jit(solution)/shard_map/ppermute | solution.py:395
  81.0 6.6 %collective-permute-start.27 = (f32[104,128]{1,0:T(8,128)S(1)}, f32[104,128]{1,0:T(8,128)S(1)}, u32[]{:S(2)}, u32[]{:S(2)}) collective-permute-start(f32[104,128]{1,0:T(8,128)S(1)} %get-tuple-element.434), channel_id=1, source_target_pairs={{0,4},{4,0},{1,5},{5,1},{2,6},{6,2},{3,7},{7,3},{8,13},{12,8},{9,1... | collective-permute-start | bytes 159752 | tf_op jit(solution)/shard_map/ppermute | solution.py:395
  93.1 5.7 %collective-permute-start.31 = (f32[104,128]{1,0:T(8,128)S(1)}, f32[104,128]{1,0:T(8,128)S(1)}, u32[]{:S(2)}, u32[]{:S(2)}) collective-permute-start(f32[104,128]{1,0:T(8,128)S(1)} %get-tuple-element.452), channel_id=1, source_target_pairs={{0,4},{4,0},{1,5},{5,1},{2,6},{6,2},{3,7},{7,3},{8,12},{12,8},{9,1... | collective-permute-start | bytes 159752 | tf_op jit(solution)/shard_map/ppermute | solution.py:395
  104.5 5.4 %collective-permute-start.35 = (f32[104,128]{1,0:T(8,128)S(1)}, f32[104,128]{1,0:T(8,128)S(1)}, u32[]{:S(2)}, u32[]{:S(2)}) collective-permute-start(f32[104,128]{1,0:T(8,128)S(1)} %get-tuple-element.470), channel_id=1, source_target_pairs={{0,4},{4,0},{1,5},{5,1},{2,6},{6,2},{3,7},{7,3},{8,12},{12,9},{9,1... | collective-permute-start | bytes 159752 | tf_op jit(solution)/shard_map/ppermute | solution.py:395
  115.3 4.2 %collective-permute-start.39 = (f32[104,128]{1,0:T(8,128)S(1)}, f32[104,128]{1,0:T(8,128)S(1)}, u32[]{:S(2)}, u32[]{:S(2)}) collective-permute-start(f32[104,128]{1,0:T(8,128)S(1)} %get-tuple-element.488), channel_id=1, source_target_pairs={{0,4},{4,1},{1,5},{5,0},{2,6},{6,3},{3,7},{7,2},{8,12},{12,9},{9,1... | collective-permute-start | bytes 159752 | tf_op jit(solution)/shard_map/ppermute | solution.py:395
  124.4 5.1 %collective-permute-start.43 = (f32[104,128]{1,0:T(8,128)S(1)}, f32[104,128]{1,0:T(8,128)S(1)}, u32[]{:S(2)}, u32[]{:S(2)}) collective-permute-start(f32[104,128]{1,0:T(8,128)S(1)} %get-tuple-element.506), channel_id=1, source_target_pairs={{0,4},{4,0},{1,5},{5,1},{2,6},{6,2},{3,7},{7,3},{8,12},{12,9},{9,1... | collective-permute-start | bytes 159752 | tf_op jit(solution)/shard_map/ppermute | solution.py:395
  133.8 5.0 %collective-permute-start.47 = (f32[104,128]{1,0:T(8,128)S(1)}, f32[104,128]{1,0:T(8,128)S(1)}, u32[]{:S(2)}, u32[]{:S(2)}) collective-permute-start(f32[104,128]{1,0:T(8,128)S(1)} %get-tuple-element.524), channel_id=1, source_target_pairs={{0,4},{4,0},{1,5},{5,1},{2,6},{6,2},{3,7},{7,3},{8,12},{12,8},{9,1... | collective-permute-start | bytes 159752 | tf_op jit(solution)/shard_map/ppermute | solution.py:395
  144.0 4.0 %collective-permute-start.51 = (f32[104,128]{1,0:T(8,128)S(1)}, f32[104,128]{1,0:T(8,128)S(1)}, u32[]{:S(2)}, u32[]{:S(2)}) collective-permute-start(f32[104,128]{1,0:T(8,128)S(1)} %get-tuple-element.542), channel_id=1, source_target_pairs={{0,4},{4,0},{1,5},{5,1},{2,6},{6,2},{3,7},{7,3},{8,13},{12,8},{9,1... | collective-permute-start | bytes 159752 | tf_op jit(solution)/shard_map/ppermute | solution.py:395
  152.4 5.4 %collective-permute-start.55 = (f32[104,128]{1,0:T(8,128)S(1)}, f32[104,128]{1,0:T(8,128)S(1)}, u32[]{:S(2)}, u32[]{:S(2)}) collective-permute-start(f32[104,128]{1,0:T(8,128)S(1)} %get-tuple-element.560), channel_id=1, source_target_pairs={{0,5},{4,0},{1,4},{5,1},{2,7},{6,2},{3,6},{7,3},{8,13},{12,8},{9,1... | collective-permute-start | bytes 159752 | tf_op jit(solution)/shard_map/ppermute | solution.py:395
  163.2 5.7 %collective-permute-start.58 = (f32[104,128]{1,0:T(8,128)S(1)}, f32[104,128]{1,0:T(8,128)S(1)}, u32[]{:S(2)}, u32[]{:S(2)}) collective-permute-start(f32[104,128]{1,0:T(8,128)S(1)} %get-tuple-element.575), channel_id=1, source_target_pairs={{0,5},{4,0},{1,4},{5,1},{2,7},{6,2},{3,6},{7,3},{8,13},{12,8},{9,1... | collective-permute-start | bytes 159752 | tf_op jit(solution)/shard_map/ppermute | solution.py:395
  168.9 3.1 %collective-permute-done.58.refs_5_ = f32[104,128]{1,0:T(8,128)S(1)} collective-permute-done((f32[104,128]{1,0:T(8,128)S(1)}, f32[104,128]{1,0:T(8,128)S(1)}, u32[]{:S(2)}, u32[]{:S(2)}) %collective-permute-start.58) | collective-permute-done | bytes 53280 | tf_op jit(solution)/shard_map/ppermute | solution.py:395
  174.1 5.2 %collective-permute-start.60 = (f32[104,128]{1,0:T(8,128)S(1)}, f32[104,128]{1,0:T(8,128)S(1)}, u32[]{:S(2)}, u32[]{:S(2)}) collective-permute-start(f32[104,128]{1,0:T(8,128)S(1)} %get-tuple-element.585), channel_id=1, source_target_pairs={{0,5},{4,0},{1,4},{5,1},{2,7},{6,2},{3,6},{7,3},{8,13},{12,8},{9,1... | collective-permute-start | bytes 159752 | tf_op jit(solution)/shard_map/ppermute | solution.py:395
  179.3 3.3 %collective-permute-done.60.refs_5_ = f32[104,128]{1,0:T(8,128)S(1)} collective-permute-done((f32[104,128]{1,0:T(8,128)S(1)}, f32[104,128]{1,0:T(8,128)S(1)}, u32[]{:S(2)}, u32[]{:S(2)}) %collective-permute-start.60) | collective-permute-done | bytes 53280 | tf_op jit(solution)/shard_map/ppermute | solution.py:395
  184.8 4.6 %collective-permute-start.62 = (f32[104,128]{1,0:T(8,128)S(1)}, f32[104,128]{1,0:T(8,128)S(1)}, u32[]{:S(2)}, u32[]{:S(2)}) collective-permute-start(f32[104,128]{1,0:T(8,128)S(1)} %get-tuple-element.595), channel_id=1, source_target_pairs={{0,5},{4,0},{1,4},{5,1},{2,7},{6,2},{3,6},{7,3},{8,12},{12,8},{9,1... | collective-permute-start | bytes 159752 | tf_op jit(solution)/shard_map/ppermute | solution.py:395
  189.4 3.3 %collective-permute-done.62.refs_5_ = f32[104,128]{1,0:T(8,128)S(1)} collective-permute-done((f32[104,128]{1,0:T(8,128)S(1)}, f32[104,128]{1,0:T(8,128)S(1)}, u32[]{:S(2)}, u32[]{:S(2)}) %collective-permute-start.62) | collective-permute-done | bytes 53280 | tf_op jit(solution)/shard_map/ppermute | solution.py:395
  (187 shorter events, 83.9 us)
Async XLA Ops:
  4.5 5.5 %collective-permute-start = (f32[104,128]{1,0:T(8,128)S(1)}, f32[104,128]{1,0:T(8,128)S(1)}, u32[]{:S(2)}, u32[]{:S(2)}) collective-permute-start(f32[104,128]{1,0:T(8,128)S(1)} %get-tuple-element.313), channel_id=1, source_target_pairs={{0,4},{4,1},{1,5},{5,0},{2,6},{6,3},{3,7},{7,2},{8,12},{12,8},{9,1... | collective-permute-start | bytes 159752 | tf_op jit(solution)/shard_map/ppermute | solution.py:395
  13.4 6.1 %collective-permute-start.2 = (f32[104,128]{1,0:T(8,128)S(1)}, f32[104,128]{1,0:T(8,128)S(1)}, u32[]{:S(2)}, u32[]{:S(2)}) collective-permute-start(f32[104,128]{1,0:T(8,128)S(1)} %get-tuple-element.323), channel_id=1, source_target_pairs={{0,4},{4,1},{1,5},{5,0},{2,6},{6,3},{3,7},{7,2},{8,12},{12,9},{9,1... | collective-permute-start | bytes 159752 | tf_op jit(solution)/shard_map/ppermute | solution.py:395
  23.0 5.0 %collective-permute-start.4 = (f32[104,128]{1,0:T(8,128)S(1)}, f32[104,128]{1,0:T(8,128)S(1)}, u32[]{:S(2)}, u32[]{:S(2)}) collective-permute-start(f32[104,128]{1,0:T(8,128)S(1)} %get-tuple-element.333), channel_id=1, source_target_pairs={{0,4},{4,1},{1,5},{5,0},{2,6},{6,3},{3,7},{7,2},{8,12},{12,9},{9,1... | collective-permute-start | bytes 159752 | tf_op jit(solution)/shard_map/ppermute | solution.py:395
  29.7 7.9 %collective-permute-start.7 = (f32[104,128]{1,0:T(8,128)S(1)}, f32[104,128]{1,0:T(8,128)S(1)}, u32[]{:S(2)}, u32[]{:S(2)}) collective-permute-start(f32[104,128]{1,0:T(8,128)S(1)} %get-tuple-element.346), channel_id=1, source_target_pairs={{0,4},{4,1},{1,5},{5,0},{2,6},{6,3},{3,7},{7,2},{8,12},{12,9},{9,1... | collective-permute-start | bytes 159752 | tf_op jit(solution)/shard_map/ppermute | solution.py:395
  38.9 9.0 %collective-permute-start.11 = (f32[104,128]{1,0:T(8,128)S(1)}, f32[104,128]{1,0:T(8,128)S(1)}, u32[]{:S(2)}, u32[]{:S(2)}) collective-permute-start(f32[104,128]{1,0:T(8,128)S(1)} %get-tuple-element.362), channel_id=1, source_target_pairs={{0,4},{4,0},{1,5},{5,1},{2,6},{6,2},{3,7},{7,3},{8,12},{12,9},{9,1... | collective-permute-start | bytes 159752 | tf_op jit(solution)/shard_map/ppermute | solution.py:395
  50.1 7.1 %collective-permute-start.15 = (f32[104,128]{1,0:T(8,128)S(1)}, f32[104,128]{1,0:T(8,128)S(1)}, u32[]{:S(2)}, u32[]{:S(2)}) collective-permute-start(f32[104,128]{1,0:T(8,128)S(1)} %get-tuple-element.380), channel_id=1, source_target_pairs={{0,4},{4,0},{1,5},{5,1},{2,6},{6,2},{3,7},{7,3},{8,12},{12,8},{9,1... | collective-permute-start | bytes 159752 | tf_op jit(solution)/shard_map/ppermute | solution.py:395
  55.0 4.5 %collective-permute-start.18 = (f32[2,104,128]{2,1,0:T(8,128)S(1)}, f32[2,104,128]{2,1,0:T(8,128)S(1)}, u32[]{:S(2)}, u32[]{:S(2)}) collective-permute-start(f32[2,104,128]{2,1,0:T(8,128)S(1)} %get-tuple-element.389), channel_id=1, source_target_pairs={{1,2},{5,6},{9,10},{13,14},{17,18},{20,21},{22,23},{25,26},{2,1},{... | collective-permute-start | bytes 319496 | tf_op jit(solution)/shard_map/ppermute | solution.py:413
  59.8 6.8 %collective-permute-start.19 = (f32[104,128]{1,0:T(8,128)S(1)}, f32[104,128]{1,0:T(8,128)S(1)}, u32[]{:S(2)}, u32[]{:S(2)}) collective-permute-start(f32[104,128]{1,0:T(8,128)S(1)} %get-tuple-element.398), channel_id=1, source_target_pairs={{0,4},{4,0},{1,5},{5,1},{2,6},{6,2},{3,7},{7,3},{8,13},{12,8},{9,1... | collective-permute-start | bytes 159752 | tf_op jit(solution)/shard_map/ppermute | solution.py:395
  68.8 8.8 %collective-permute-start.23 = (f32[104,128]{1,0:T(8,128)S(1)}, f32[104,128]{1,0:T(8,128)S(1)}, u32[]{:S(2)}, u32[]{:S(2)}) collective-permute-start(f32[104,128]{1,0:T(8,128)S(1)} %get-tuple-element.416), channel_id=1, source_target_pairs={{0,5},{4,0},{1,4},{5,1},{2,7},{6,2},{3,6},{7,3},{8,13},{12,8},{9,1... | collective-permute-start | bytes 159752 | tf_op jit(solution)/shard_map/ppermute | solution.py:395
  74.5 4.8 %collective-permute-start.26 = (f32[2,104,128]{2,1,0:T(8,128)S(1)}, f32[2,104,128]{2,1,0:T(8,128)S(1)}, u32[]{:S(2)}, u32[]{:S(2)}) collective-permute-start(f32[2,104,128]{2,1,0:T(8,128)S(1)} %get-tuple-element.425), channel_id=1, source_target_pairs={{1,2},{5,6},{8,9},{10,11},{13,14},{17,18},{20,21},{22,23},{24,25},... | collective-permute-start | bytes 319496 | tf_op jit(solution)/shard_map/ppermute | solution.py:413
  81.0 9.0 %collective-permute-start.27 = (f32[104,128]{1,0:T(8,128)S(1)}, f32[104,128]{1,0:T(8,128)S(1)}, u32[]{:S(2)}, u32[]{:S(2)}) collective-permute-start(f32[104,128]{1,0:T(8,128)S(1)} %get-tuple-element.434), channel_id=1, source_target_pairs={{0,4},{4,0},{1,5},{5,1},{2,6},{6,2},{3,7},{7,3},{8,13},{12,8},{9,1... | collective-permute-start | bytes 159752 | tf_op jit(solution)/shard_map/ppermute | solution.py:395
  93.1 8.3 %collective-permute-start.31 = (f32[104,128]{1,0:T(8,128)S(1)}, f32[104,128]{1,0:T(8,128)S(1)}, u32[]{:S(2)}, u32[]{:S(2)}) collective-permute-start(f32[104,128]{1,0:T(8,128)S(1)} %get-tuple-element.452), channel_id=1, source_target_pairs={{0,4},{4,0},{1,5},{5,1},{2,6},{6,2},{3,7},{7,3},{8,12},{12,8},{9,1... | collective-permute-start | bytes 159752 | tf_op jit(solution)/shard_map/ppermute | solution.py:395
  104.5 7.7 %collective-permute-start.35 = (f32[104,128]{1,0:T(8,128)S(1)}, f32[104,128]{1,0:T(8,128)S(1)}, u32[]{:S(2)}, u32[]{:S(2)}) collective-permute-start(f32[104,128]{1,0:T(8,128)S(1)} %get-tuple-element.470), channel_id=1, source_target_pairs={{0,4},{4,0},{1,5},{5,1},{2,6},{6,2},{3,7},{7,3},{8,12},{12,9},{9,1... | collective-permute-start | bytes 159752 | tf_op jit(solution)/shard_map/ppermute | solution.py:395
  115.3 6.2 %collective-permute-start.39 = (f32[104,128]{1,0:T(8,128)S(1)}, f32[104,128]{1,0:T(8,128)S(1)}, u32[]{:S(2)}, u32[]{:S(2)}) collective-permute-start(f32[104,128]{1,0:T(8,128)S(1)} %get-tuple-element.488), channel_id=1, source_target_pairs={{0,4},{4,1},{1,5},{5,0},{2,6},{6,3},{3,7},{7,2},{8,12},{12,9},{9,1... | collective-permute-start | bytes 159752 | tf_op jit(solution)/shard_map/ppermute | solution.py:395
  119.4 4.8 %collective-permute-start.42 = (f32[2,104,128]{2,1,0:T(8,128)S(1)}, f32[2,104,128]{2,1,0:T(8,128)S(1)}, u32[]{:S(2)}, u32[]{:S(2)}) collective-permute-start(f32[2,104,128]{2,1,0:T(8,128)S(1)} %get-tuple-element.497), channel_id=1, source_target_pairs={{4,5},{6,7},{8,9},{10,11},{13,14},{17,18},{20,21},{22,23},{25,26},... | collective-permute-start | bytes 319496 | tf_op jit(solution)/shard_map/ppermute | solution.py:413
  124.4 7.6 %collective-permute-start.43 = (f32[104,128]{1,0:T(8,128)S(1)}, f32[104,128]{1,0:T(8,128)S(1)}, u32[]{:S(2)}, u32[]{:S(2)}) collective-permute-start(f32[104,128]{1,0:T(8,128)S(1)} %get-tuple-element.506), channel_id=1, source_target_pairs={{0,4},{4,0},{1,5},{5,1},{2,6},{6,2},{3,7},{7,3},{8,12},{12,9},{9,1... | collective-permute-start | bytes 159752 | tf_op jit(solution)/shard_map/ppermute | solution.py:395
  133.8 7.2 %collective-permute-start.47 = (f32[104,128]{1,0:T(8,128)S(1)}, f32[104,128]{1,0:T(8,128)S(1)}, u32[]{:S(2)}, u32[]{:S(2)}) collective-permute-start(f32[104,128]{1,0:T(8,128)S(1)} %get-tuple-element.524), channel_id=1, source_target_pairs={{0,4},{4,0},{1,5},{5,1},{2,6},{6,2},{3,7},{7,3},{8,12},{12,8},{9,1... | collective-permute-start | bytes 159752 | tf_op jit(solution)/shard_map/ppermute | solution.py:395
  138.9 4.9 %collective-permute-start.50 = (f32[2,104,128]{2,1,0:T(8,128)S(1)}, f32[2,104,128]{2,1,0:T(8,128)S(1)}, u32[]{:S(2)}, u32[]{:S(2)}) collective-permute-start(f32[2,104,128]{2,1,0:T(8,128)S(1)} %get-tuple-element.533), channel_id=1, source_target_pairs={{1,2},{5,6},{8,9},{10,11},{13,14},{17,18},{20,21},{22,23},{25,26},... | collective-permute-start | bytes 319496 | tf_op jit(solution)/shard_map/ppermute | solution.py:413
  144.0 6.2 %collective-permute-start.51 = (f32[104,128]{1,0:T(8,128)S(1)}, f32[104,128]{1,0:T(8,128)S(1)}, u32[]{:S(2)}, u32[]{:S(2)}) collective-permute-start(f32[104,128]{1,0:T(8,128)S(1)} %get-tuple-element.542), channel_id=1, source_target_pairs={{0,4},{4,0},{1,5},{5,1},{2,6},{6,2},{3,7},{7,3},{8,13},{12,8},{9,1... | collective-permute-start | bytes 159752 | tf_op jit(solution)/shard_map/ppermute | solution.py:395
  152.4 8.4 %collective-permute-start.55 = (f32[104,128]{1,0:T(8,128)S(1)}, f32[104,128]{1,0:T(8,128)S(1)}, u32[]{:S(2)}, u32[]{:S(2)}) collective-permute-start(f32[104,128]{1,0:T(8,128)S(1)} %get-tuple-element.560), channel_id=1, source_target_pairs={{0,5},{4,0},{1,4},{5,1},{2,7},{6,2},{3,6},{7,3},{8,13},{12,8},{9,1... | collective-permute-start | bytes 159752 | tf_op jit(solution)/shard_map/ppermute | solution.py:395
  157.7 4.6 %collective-permute-start.57 = (f32[2,104,128]{2,1,0:T(8,128)S(1)}, f32[2,104,128]{2,1,0:T(8,128)S(1)}, u32[]{:S(2)}, u32[]{:S(2)}) collective-permute-start(f32[2,104,128]{2,1,0:T(8,128)S(1)} %get-tuple-element.568), channel_id=1, source_target_pairs={{1,2},{8,9},{10,11},{20,21},{22,23},{2,1},{9,8},{11,10},{21,20},{2... | collective-permute-start | bytes 319496 | tf_op jit(solution)/shard_map/ppermute | solution.py:413
  163.2 8.7 %collective-permute-start.58 = (f32[104,128]{1,0:T(8,128)S(1)}, f32[104,128]{1,0:T(8,128)S(1)}, u32[]{:S(2)}, u32[]{:S(2)}) collective-permute-start(f32[104,128]{1,0:T(8,128)S(1)} %get-tuple-element.575), channel_id=1, source_target_pairs={{0,5},{4,0},{1,4},{5,1},{2,7},{6,2},{3,6},{7,3},{8,13},{12,8},{9,1... | collective-permute-start | bytes 159752 | tf_op jit(solution)/shard_map/ppermute | solution.py:395
  174.1 8.5 %collective-permute-start.60 = (f32[104,128]{1,0:T(8,128)S(1)}, f32[104,128]{1,0:T(8,128)S(1)}, u32[]{:S(2)}, u32[]{:S(2)}) collective-permute-start(f32[104,128]{1,0:T(8,128)S(1)} %get-tuple-element.585), channel_id=1, source_target_pairs={{0,5},{4,0},{1,4},{5,1},{2,7},{6,2},{3,6},{7,3},{8,13},{12,8},{9,1... | collective-permute-start | bytes 159752 | tf_op jit(solution)/shard_map/ppermute | solution.py:395
  184.8 7.9 %collective-permute-start.62 = (f32[104,128]{1,0:T(8,128)S(1)}, f32[104,128]{1,0:T(8,128)S(1)}, u32[]{:S(2)}, u32[]{:S(2)}) collective-permute-start(f32[104,128]{1,0:T(8,128)S(1)} %get-tuple-element.595), channel_id=1, source_target_pairs={{0,5},{4,0},{1,4},{5,1},{2,7},{6,2},{3,6},{7,3},{8,12},{12,8},{9,1... | collective-permute-start | bytes 159752 | tf_op jit(solution)/shard_map/ppermute | solution.py:395
  (40 other events, 82.0 us)

commit v3 on v2

--- a/solution.py
+++ b/solution.py
@@ -127,28 +127,30 @@
         base[vector] = base[vector] - product(blocks.at[jnp.where(on_right, RIGHT, LEFT)], spare, spare.shape[0])
 
 
-def prepare(block, ready, narrow, wide, sems):
+def prepare(block, ready, narrow, wide, sems, low, high):
     size, _, lanes = block.shape
     rows = ready.shape[1]
-    share = size // CHUNKS
+    bounds = [low + (high - low) * n // CHUNKS for n in range(CHUNKS + 1)]
+    shares = list(zip(bounds, bounds[1:]))
     copies = [
-        pltpu.make_async_copy(block.at[pl.ds(n * share, share)], narrow.at[pl.ds(n * share, share)], sems.at[n])
-        for n in range(CHUNKS)
+        pltpu.make_async_copy(block.at[pl.ds(a, b - a)], narrow.at[pl.ds(a, b - a)], sems.at[n])
+        for n, (a, b) in enumerate(shares)
     ]
     for copy in copies:
         copy.start()
-    wide[pl.ds(size * rows, (rows - size) * rows), :] = jnp.zeros(((rows - size) * rows, lanes), jnp.float32)
+    if high == size:
+        wide[pl.ds(size * rows, (rows - size) * rows), :] = jnp.zeros(((rows - size) * rows, lanes), jnp.float32)
 
     def widen(i, _):
         wide[pl.ds(pl.multiple_of(i * rows, SUBLANES), size), :] = narrow[i].astype(jnp.float32)
         return 0
 
-    for n, copy in enumerate(copies):
+    for (a, b), copy in zip(shares, copies):
         copy.wait()
-        lax.fori_loop(n * share, (n + 1) * share, widen, 0, unroll=5)
+        lax.fori_loop(a, b, widen, 0, unroll=next(n for n in (5, 4, 1) if (b - a) % n == 0))
 
     def turn(j, _):
-        for i in range(0, rows, SUBLANES):
+        for i in range(low, high, SUBLANES):
             ready[j, pl.ds(i, SUBLANES), :] = wide[pl.ds(i * rows + j, SUBLANES, stride=rows), :]
         return 0
 
@@ -156,29 +158,29 @@
 
 
 def first_kernel(block, residual, *refs):
-    hbm_columns, (blocks, base, source, blank, *columns), (narrow, wide, sems, column_sems) = (
+    hbm_columns, (blocks, base, source, blank, *columns), (narrow, wide, sems, column_sems, held_residual) = (
         refs[:4], refs[4:12], refs[12:]
     )
     copies = [
         pltpu.make_async_copy(there, here, column_sems.at[n])
-        for n, (there, here) in enumerate(zip(hbm_columns, columns))
+        for n, (there, here) in enumerate(zip((*hbm_columns, residual), (*columns, held_residual)))
     ]
     for copy in copies:
         copy.start()
-    prepare(block, blocks.at[DIAG], narrow, wide, sems)
     size, vectors, lanes = residual.shape
+    prepare(block, blocks.at[DIAG], narrow, wide, sems, 0, size)
+    for copy in copies:
+        copy.wait()
     rows = base.shape[1]
     base[:, pl.ds(rows - SUBLANES, SUBLANES), :] = jnp.zeros((vectors, SUBLANES, lanes), jnp.float32)
     for vector in range(vectors):
-        base[vector, pl.ds(0, size), :] = residual[:, vector, :]
+        base[vector, pl.ds(0, size), :] = held_residual[:, vector, :]
     source[...] = base[...]
     blank[...] = jnp.zeros_like(blank)
-    for copy in copies:
-        copy.wait()
-
-
-def later_kernel(face, slot, block, blocks_in, blocks, narrow, wide, sems):
-    prepare(block.at[(0,) * (len(block.shape) - 4) + (face,)], blocks.at[slot], narrow, wide, sems)
+
+
+def later_kernel(face, slot, low, high, block, blocks_in, blocks, narrow, wide, sems):
+    prepare(block.at[(0,) * (len(block.shape) - 4) + (face,)], blocks.at[slot], narrow, wide, sems, low, high)
 
 
 def task_kernel(
@@ -312,17 +314,19 @@
             held((5, size, rows, lanes)), held(several), held(several), held((rows, lanes)),
             *(pltpu.VMEM(one.shape, one.dtype) for one in columns),
         ),
-        in_specs=[in_hbm, *in_vmem(1), *[in_hbm] * 4],
+        in_specs=[in_hbm] * 6,
         out_specs=tuple(in_vmem(8)),
-        scratch_shapes=[*preparing(size, rows, lanes), pltpu.SemaphoreType.DMA((4,))],
+        scratch_shapes=[
+            *preparing(size, rows, lanes), pltpu.SemaphoreType.DMA((5,)), held((size, vectors, lanes))
+        ],
         compiler_params=pltpu.CompilerParams(vmem_limit_bytes=PREPARE_LIMIT),
         name="first",
-    )(far(block), residual, *(far(one) for one in columns))
-
-
-def later_call(block, face, slot, blocks):
+    )(far(block), far(residual), *(far(one) for one in columns))
+
+
+def later_call(blocks, block, face, slot, low, high):
     return pl.pallas_call(
-        functools.partial(later_kernel, face, slot),
+        functools.partial(later_kernel, face, slot, low, high),
         out_shape=held(blocks.shape),
         in_specs=[pl.BlockSpec(memory_space=pltpu.HBM), *in_vmem(1)],
         out_specs=in_vmem(1)[0],
@@ -363,7 +367,10 @@
         name="room",
     )()
     incoming = arrived = blank
-    late_blocks = [(up_block, 0, UP), *((side_blocks, face, DOWN + face) for face in range(3))]
+    middle = size // 2 // SUBLANES * SUBLANES
+    late_blocks = [(up_block, 0, UP, 0, size)]
+    for slot in (LEFT, RIGHT, DOWN):
+        late_blocks += [(side_blocks, slot - DOWN, slot, 0, middle), (side_blocks, slot - DOWN, slot, middle, size)]
 
     def tasks_at(tick):
         return [task_at(tick, place, count, vectors, lambda which, a, b: a if which else b) for place in range(count)]
@@ -421,7 +428,7 @@
                 (rows, lanes),
             )
         if tick < len(late_blocks):
-            blocks = later_call(*late_blocks[tick], blocks)
+            blocks = later_call(blocks, *late_blocks[tick])
     return out[None, None]
 
 

time: 196 us -> 196 us (level)
  Pallas kernels: 32.8 us -> 36 us
  waiting for transfers between devices: 34 us -> 32 us
    pallas_call x4 -> x7, Pallas kernels: 11.5 us -> 14.5 us  [later_call(): pl.pallas_call(functools.partial(later_kernel, face, slot, low, high), ou...]
    ppermute x37, waiting for transfers between devices: 33.9 us -> 31.9 us  [per_device(): incoming = lax.ppermute(value, ('sweep', 'span'), pairs)]
  transfers between devices with their start and end apart: 63 -> 63, of which waited for: 29 -> 26; matrix products, arithmetic and copies ran while one was open for 0% -> 0% of each run, Pallas kernels for 11% -> 13%
where the time goes in v3:
time: 196 us; the launch traced here: 195 us
  starting transfers between devices  125 us (64%)
  Pallas kernels  36 us (18%)
  waiting for transfers between devices  32 us (16%)
    ppermute x37, starting transfers between devices, per_device(): incoming = lax.ppermute(value, ('sweep', 'span'), pairs)  103 us
    ppermute x37, waiting for transfers between devices, per_device(): incoming = lax.ppermute(value, ('sweep', 'span'), pairs)  31.9 us
    ppermute x26, starting transfers between devices, per_device(): lax.ppermute(cross[0], ('sweep', 'span'), closed(pairs, range(count * par...  22.2 us
    pallas_call x76, Pallas kernels, call(): pl.pallas_call(body, out_shape=tuple((held(shape) for shape in [*(a.shape...  18.4 us
    pallas_call x7, Pallas kernels, later_call(): pl.pallas_call(functools.partial(later_kernel, face, slot, low, high), ou...  14.5 us
  transfers between devices with their start and end apart: 63, of which 26 were waited for; matrix products, arithmetic and copies ran while one was open for 0% of the time, Pallas kernels for 13%

profile of v3, /device:TPU:0, one launch (start us, length us, event | category | flops | bytes accessed | tf_op | source)
XLA Modules:
  0.0 195.0 jit_solution(1979744997440234875)
XLA Ops:
  0.0 3.2 %first.1 = (f32[5,100,104,128]{3,2,1,0:T(8,128)S(1)}, f32[4,104,128]{2,1,0:T(8,128)S(1)}, f32[4,104,128]{2,1,0:T(8,128)S(1)}, f32[104,128]{1,0:T(8,128)S(1)}, s3...) custom-call(bf16[100,100,128]{2,1,0:T(8,128)(2,1)} %bitcast.10, ...), custom_call_target="tpu_custom_call" | custom-call | tf_op jit(solution)/shard_map/first/pallas_call | solution.py:311
  3.6 2.6 %collective-permute-start = (f32[104,128]{1,0:T(8,128)S(1)}, f32[104,128]{1,0:T(8,128)S(1)}, u32[]{:S(2)}, u32[]{:S(2)}) collective-permute-start(f32[104,128]{1,0:T(8,128)S(1)} %get-tuple-element.313), channel_id=1, source_target_pairs={{0,4},{4,1},{1,5},{5,0},{2,6},{6,3},{3,7},{7,2},{8,12},{12,8},{9,1... | collective-permute-start | bytes 159752 | tf_op jit(solution)/shard_map/ppermute | solution.py:402
  6.2 2.9 %later.7.refs_7_ = f32[5,100,104,128]{3,2,1,0:T(8,128)S(1)} custom-call(bf16[1,1,100,100,128]{4,3,2,1,0:T(8,128)(2,1)} %block.7, f32[5,100,104,128]{3,2,1,0:T(8,128)S(1)} %get-tuple-element.314.blocks_in), custom_call_target="tpu_custom_call", output_to_operand_aliasing={{}: (1, {})} | custom-call | tf_op jit(solution)/shard_map/later/pallas_call | solution.py:328
  11.5 4.2 %collective-permute-start.2 = (f32[104,128]{1,0:T(8,128)S(1)}, f32[104,128]{1,0:T(8,128)S(1)}, u32[]{:S(2)}, u32[]{:S(2)}) collective-permute-start(f32[104,128]{1,0:T(8,128)S(1)} %get-tuple-element.323), channel_id=1, source_target_pairs={{0,4},{4,1},{1,5},{5,0},{2,6},{6,3},{3,7},{7,2},{8,12},{12,9},{9,1... | collective-permute-start | bytes 159752 | tf_op jit(solution)/shard_map/ppermute | solution.py:402
  20.2 5.1 %collective-permute-start.4 = (f32[104,128]{1,0:T(8,128)S(1)}, f32[104,128]{1,0:T(8,128)S(1)}, u32[]{:S(2)}, u32[]{:S(2)}) collective-permute-start(f32[104,128]{1,0:T(8,128)S(1)} %get-tuple-element.333), channel_id=1, source_target_pairs={{0,4},{4,1},{1,5},{5,0},{2,6},{6,3},{3,7},{7,2},{8,12},{12,9},{9,1... | collective-permute-start | bytes 159752 | tf_op jit(solution)/shard_map/ppermute | solution.py:402
  30.5 5.0 %collective-permute-start.7 = (f32[104,128]{1,0:T(8,128)S(1)}, f32[104,128]{1,0:T(8,128)S(1)}, u32[]{:S(2)}, u32[]{:S(2)}) collective-permute-start(f32[104,128]{1,0:T(8,128)S(1)} %get-tuple-element.346), channel_id=1, source_target_pairs={{0,4},{4,1},{1,5},{5,0},{2,6},{6,3},{3,7},{7,2},{8,12},{12,9},{9,1... | collective-permute-start | bytes 159752 | tf_op jit(solution)/shard_map/ppermute | solution.py:402
  39.5 7.9 %collective-permute-start.11 = (f32[104,128]{1,0:T(8,128)S(1)}, f32[104,128]{1,0:T(8,128)S(1)}, u32[]{:S(2)}, u32[]{:S(2)}) collective-permute-start(f32[104,128]{1,0:T(8,128)S(1)} %get-tuple-element.362), channel_id=1, source_target_pairs={{0,4},{4,0},{1,5},{5,1},{2,6},{6,2},{3,7},{7,3},{8,12},{12,9},{9,1... | collective-permute-start | bytes 159752 | tf_op jit(solution)/shard_map/ppermute | solution.py:402
  51.7 4.9 %collective-permute-start.15 = (f32[104,128]{1,0:T(8,128)S(1)}, f32[104,128]{1,0:T(8,128)S(1)}, u32[]{:S(2)}, u32[]{:S(2)}) collective-permute-start(f32[104,128]{1,0:T(8,128)S(1)} %get-tuple-element.380), channel_id=1, source_target_pairs={{0,4},{4,0},{1,5},{5,1},{2,6},{6,2},{3,7},{7,3},{8,12},{12,8},{9,1... | collective-permute-start | bytes 159752 | tf_op jit(solution)/shard_map/ppermute | solution.py:402
  60.1 5.8 %collective-permute-start.19 = (f32[104,128]{1,0:T(8,128)S(1)}, f32[104,128]{1,0:T(8,128)S(1)}, u32[]{:S(2)}, u32[]{:S(2)}) collective-permute-start(f32[104,128]{1,0:T(8,128)S(1)} %get-tuple-element.398), channel_id=1, source_target_pairs={{0,4},{4,0},{1,5},{5,1},{2,6},{6,2},{3,7},{7,3},{8,13},{12,8},{9,1... | collective-permute-start | bytes 159752 | tf_op jit(solution)/shard_map/ppermute | solution.py:402
  70.2 5.4 %collective-permute-start.23 = (f32[104,128]{1,0:T(8,128)S(1)}, f32[104,128]{1,0:T(8,128)S(1)}, u32[]{:S(2)}, u32[]{:S(2)}) collective-permute-start(f32[104,128]{1,0:T(8,128)S(1)} %get-tuple-element.416), channel_id=1, source_target_pairs={{0,5},{4,0},{1,4},{5,1},{2,7},{6,2},{3,6},{7,3},{8,13},{12,8},{9,1... | collective-permute-start | bytes 159752 | tf_op jit(solution)/shard_map/ppermute | solution.py:402
  82.0 5.6 %collective-permute-start.27 = (f32[104,128]{1,0:T(8,128)S(1)}, f32[104,128]{1,0:T(8,128)S(1)}, u32[]{:S(2)}, u32[]{:S(2)}) collective-permute-start(f32[104,128]{1,0:T(8,128)S(1)} %get-tuple-element.434), channel_id=1, source_target_pairs={{0,4},{4,0},{1,5},{5,1},{2,6},{6,2},{3,7},{7,3},{8,13},{12,8},{9,1... | collective-permute-start | bytes 159752 | tf_op jit(solution)/shard_map/ppermute | solution.py:402
  93.3 5.6 %collective-permute-start.31 = (f32[104,128]{1,0:T(8,128)S(1)}, f32[104,128]{1,0:T(8,128)S(1)}, u32[]{:S(2)}, u32[]{:S(2)}) collective-permute-start(f32[104,128]{1,0:T(8,128)S(1)} %get-tuple-element.452), channel_id=1, source_target_pairs={{0,4},{4,0},{1,5},{5,1},{2,6},{6,2},{3,7},{7,3},{8,12},{12,8},{9,1... | collective-permute-start | bytes 159752 | tf_op jit(solution)/shard_map/ppermute | solution.py:402
  104.5 5.8 %collective-permute-start.35 = (f32[104,128]{1,0:T(8,128)S(1)}, f32[104,128]{1,0:T(8,128)S(1)}, u32[]{:S(2)}, u32[]{:S(2)}) collective-permute-start(f32[104,128]{1,0:T(8,128)S(1)} %get-tuple-element.470), channel_id=1, source_target_pairs={{0,4},{4,0},{1,5},{5,1},{2,6},{6,2},{3,7},{7,3},{8,12},{12,9},{9,1... | collective-permute-start | bytes 159752 | tf_op jit(solution)/shard_map/ppermute | solution.py:402
  116.1 3.9 %collective-permute-start.39 = (f32[104,128]{1,0:T(8,128)S(1)}, f32[104,128]{1,0:T(8,128)S(1)}, u32[]{:S(2)}, u32[]{:S(2)}) collective-permute-start(f32[104,128]{1,0:T(8,128)S(1)} %get-tuple-element.488), channel_id=1, source_target_pairs={{0,4},{4,1},{1,5},{5,0},{2,6},{6,3},{3,7},{7,2},{8,12},{12,9},{9,1... | collective-permute-start | bytes 159752 | tf_op jit(solution)/shard_map/ppermute | solution.py:402
  125.3 5.1 %collective-permute-start.43 = (f32[104,128]{1,0:T(8,128)S(1)}, f32[104,128]{1,0:T(8,128)S(1)}, u32[]{:S(2)}, u32[]{:S(2)}) collective-permute-start(f32[104,128]{1,0:T(8,128)S(1)} %get-tuple-element.506), channel_id=1, source_target_pairs={{0,4},{4,0},{1,5},{5,1},{2,6},{6,2},{3,7},{7,3},{8,12},{12,9},{9,1... | collective-permute-start | bytes 159752 | tf_op jit(solution)/shard_map/ppermute | solution.py:402
  134.7 5.0 %collective-permute-start.47 = (f32[104,128]{1,0:T(8,128)S(1)}, f32[104,128]{1,0:T(8,128)S(1)}, u32[]{:S(2)}, u32[]{:S(2)}) collective-permute-start(f32[104,128]{1,0:T(8,128)S(1)} %get-tuple-element.524), channel_id=1, source_target_pairs={{0,4},{4,0},{1,5},{5,1},{2,6},{6,2},{3,7},{7,3},{8,12},{12,8},{9,1... | collective-permute-start | bytes 159752 | tf_op jit(solution)/shard_map/ppermute | solution.py:402
  145.0 3.9 %collective-permute-start.51 = (f32[104,128]{1,0:T(8,128)S(1)}, f32[104,128]{1,0:T(8,128)S(1)}, u32[]{:S(2)}, u32[]{:S(2)}) collective-permute-start(f32[104,128]{1,0:T(8,128)S(1)} %get-tuple-element.542), channel_id=1, source_target_pairs={{0,4},{4,0},{1,5},{5,1},{2,6},{6,2},{3,7},{7,3},{8,13},{12,8},{9,1... | collective-permute-start | bytes 159752 | tf_op jit(solution)/shard_map/ppermute | solution.py:402
  153.4 4.6 %collective-permute-start.55 = (f32[104,128]{1,0:T(8,128)S(1)}, f32[104,128]{1,0:T(8,128)S(1)}, u32[]{:S(2)}, u32[]{:S(2)}) collective-permute-start(f32[104,128]{1,0:T(8,128)S(1)} %get-tuple-element.560), channel_id=1, source_target_pairs={{0,5},{4,0},{1,4},{5,1},{2,7},{6,2},{3,6},{7,3},{8,13},{12,8},{9,1... | collective-permute-start | bytes 159752 | tf_op jit(solution)/shard_map/ppermute | solution.py:402
  163.5 5.3 %collective-permute-start.58 = (f32[104,128]{1,0:T(8,128)S(1)}, f32[104,128]{1,0:T(8,128)S(1)}, u32[]{:S(2)}, u32[]{:S(2)}) collective-permute-start(f32[104,128]{1,0:T(8,128)S(1)} %get-tuple-element.575), channel_id=1, source_target_pairs={{0,5},{4,0},{1,4},{5,1},{2,7},{6,2},{3,6},{7,3},{8,13},{12,8},{9,1... | collective-permute-start | bytes 159752 | tf_op jit(solution)/shard_map/ppermute | solution.py:402
  168.8 3.0 %collective-permute-done.58.refs_5_ = f32[104,128]{1,0:T(8,128)S(1)} collective-permute-done((f32[104,128]{1,0:T(8,128)S(1)}, f32[104,128]{1,0:T(8,128)S(1)}, u32[]{:S(2)}, u32[]{:S(2)}) %collective-permute-start.58) | collective-permute-done | bytes 53280 | tf_op jit(solution)/shard_map/ppermute | solution.py:402
  174.0 5.4 %collective-permute-start.60 = (f32[104,128]{1,0:T(8,128)S(1)}, f32[104,128]{1,0:T(8,128)S(1)}, u32[]{:S(2)}, u32[]{:S(2)}) collective-permute-start(f32[104,128]{1,0:T(8,128)S(1)} %get-tuple-element.585), channel_id=1, source_target_pairs={{0,5},{4,0},{1,4},{5,1},{2,7},{6,2},{3,6},{7,3},{8,13},{12,8},{9,1... | collective-permute-start | bytes 159752 | tf_op jit(solution)/shard_map/ppermute | solution.py:402
  179.4 3.3 %collective-permute-done.60.refs_5_ = f32[104,128]{1,0:T(8,128)S(1)} collective-permute-done((f32[104,128]{1,0:T(8,128)S(1)}, f32[104,128]{1,0:T(8,128)S(1)}, u32[]{:S(2)}, u32[]{:S(2)}) %collective-permute-start.60) | collective-permute-done | bytes 53280 | tf_op jit(solution)/shard_map/ppermute | solution.py:402
  184.9 4.6 %collective-permute-start.62 = (f32[104,128]{1,0:T(8,128)S(1)}, f32[104,128]{1,0:T(8,128)S(1)}, u32[]{:S(2)}, u32[]{:S(2)}) collective-permute-start(f32[104,128]{1,0:T(8,128)S(1)} %get-tuple-element.595), channel_id=1, source_target_pairs={{0,5},{4,0},{1,4},{5,1},{2,7},{6,2},{3,6},{7,3},{8,12},{12,8},{9,1... | collective-permute-start | bytes 159752 | tf_op jit(solution)/shard_map/ppermute | solution.py:402
  189.5 3.3 %collective-permute-done.62.refs_5_ = f32[104,128]{1,0:T(8,128)S(1)} collective-permute-done((f32[104,128]{1,0:T(8,128)S(1)}, f32[104,128]{1,0:T(8,128)S(1)}, u32[]{:S(2)}, u32[]{:S(2)}) %collective-permute-start.62) | collective-permute-done | bytes 53280 | tf_op jit(solution)/shard_map/ppermute | solution.py:402
  (188 shorter events, 82.4 us)
Async XLA Ops:
  3.6 5.5 %collective-permute-start = (f32[104,128]{1,0:T(8,128)S(1)}, f32[104,128]{1,0:T(8,128)S(1)}, u32[]{:S(2)}, u32[]{:S(2)}) collective-permute-start(f32[104,128]{1,0:T(8,128)S(1)} %get-tuple-element.313), channel_id=1, source_target_pairs={{0,4},{4,1},{1,5},{5,0},{2,6},{6,3},{3,7},{7,2},{8,12},{12,8},{9,1... | collective-permute-start | bytes 159752 | tf_op jit(solution)/shard_map/ppermute | solution.py:402
  11.5 6.2 %collective-permute-start.2 = (f32[104,128]{1,0:T(8,128)S(1)}, f32[104,128]{1,0:T(8,128)S(1)}, u32[]{:S(2)}, u32[]{:S(2)}) collective-permute-start(f32[104,128]{1,0:T(8,128)S(1)} %get-tuple-element.323), channel_id=1, source_target_pairs={{0,4},{4,1},{1,5},{5,0},{2,6},{6,3},{3,7},{7,2},{8,12},{12,9},{9,1... | collective-permute-start | bytes 159752 | tf_op jit(solution)/shard_map/ppermute | solution.py:402
  20.2 7.8 %collective-permute-start.4 = (f32[104,128]{1,0:T(8,128)S(1)}, f32[104,128]{1,0:T(8,128)S(1)}, u32[]{:S(2)}, u32[]{:S(2)}) collective-permute-start(f32[104,128]{1,0:T(8,128)S(1)} %get-tuple-element.333), channel_id=1, source_target_pairs={{0,4},{4,1},{1,5},{5,0},{2,6},{6,3},{3,7},{7,2},{8,12},{12,9},{9,1... | collective-permute-start | bytes 159752 | tf_op jit(solution)/shard_map/ppermute | solution.py:402
  30.5 7.6 %collective-permute-start.7 = (f32[104,128]{1,0:T(8,128)S(1)}, f32[104,128]{1,0:T(8,128)S(1)}, u32[]{:S(2)}, u32[]{:S(2)}) collective-permute-start(f32[104,128]{1,0:T(8,128)S(1)} %get-tuple-element.346), channel_id=1, source_target_pairs={{0,4},{4,1},{1,5},{5,0},{2,6},{6,3},{3,7},{7,2},{8,12},{12,9},{9,1... | collective-permute-start | bytes 159752 | tf_op jit(solution)/shard_map/ppermute | solution.py:402
  39.5 10.0 %collective-permute-start.11 = (f32[104,128]{1,0:T(8,128)S(1)}, f32[104,128]{1,0:T(8,128)S(1)}, u32[]{:S(2)}, u32[]{:S(2)}) collective-permute-start(f32[104,128]{1,0:T(8,128)S(1)} %get-tuple-element.362), channel_id=1, source_target_pairs={{0,4},{4,0},{1,5},{5,1},{2,6},{6,2},{3,7},{7,3},{8,12},{12,9},{9,1... | collective-permute-start | bytes 159752 | tf_op jit(solution)/shard_map/ppermute | solution.py:402
  51.7 7.1 %collective-permute-start.15 = (f32[104,128]{1,0:T(8,128)S(1)}, f32[104,128]{1,0:T(8,128)S(1)}, u32[]{:S(2)}, u32[]{:S(2)}) collective-permute-start(f32[104,128]{1,0:T(8,128)S(1)} %get-tuple-element.380), channel_id=1, source_target_pairs={{0,4},{4,0},{1,5},{5,1},{2,6},{6,2},{3,7},{7,3},{8,12},{12,8},{9,1... | collective-permute-start | bytes 159752 | tf_op jit(solution)/shard_map/ppermute | solution.py:402
  60.1 7.9 %collective-permute-start.19 = (f32[104,128]{1,0:T(8,128)S(1)}, f32[104,128]{1,0:T(8,128)S(1)}, u32[]{:S(2)}, u32[]{:S(2)}) collective-permute-start(f32[104,128]{1,0:T(8,128)S(1)} %get-tuple-element.398), channel_id=1, source_target_pairs={{0,4},{4,0},{1,5},{5,1},{2,6},{6,2},{3,7},{7,3},{8,13},{12,8},{9,1... | collective-permute-start | bytes 159752 | tf_op jit(solution)/shard_map/ppermute | solution.py:402
  70.2 8.5 %collective-permute-start.23 = (f32[104,128]{1,0:T(8,128)S(1)}, f32[104,128]{1,0:T(8,128)S(1)}, u32[]{:S(2)}, u32[]{:S(2)}) collective-permute-start(f32[104,128]{1,0:T(8,128)S(1)} %get-tuple-element.416), channel_id=1, source_target_pairs={{0,5},{4,0},{1,4},{5,1},{2,7},{6,2},{3,6},{7,3},{8,13},{12,8},{9,1... | collective-permute-start | bytes 159752 | tf_op jit(solution)/shard_map/ppermute | solution.py:402
  75.6 4.8 %collective-permute-start.26 = (f32[2,104,128]{2,1,0:T(8,128)S(1)}, f32[2,104,128]{2,1,0:T(8,128)S(1)}, u32[]{:S(2)}, u32[]{:S(2)}) collective-permute-start(f32[2,104,128]{2,1,0:T(8,128)S(1)} %get-tuple-element.425), channel_id=1, source_target_pairs={{1,2},{5,6},{8,9},{10,11},{13,14},{17,18},{20,21},{22,23},{24,25},... | collective-permute-start | bytes 319496 | tf_op jit(solution)/shard_map/ppermute | solution.py:420
  82.0 8.2 %collective-permute-start.27 = (f32[104,128]{1,0:T(8,128)S(1)}, f32[104,128]{1,0:T(8,128)S(1)}, u32[]{:S(2)}, u32[]{:S(2)}) collective-permute-start(f32[104,128]{1,0:T(8,128)S(1)} %get-tuple-element.434), channel_id=1, source_target_pairs={{0,4},{4,0},{1,5},{5,1},{2,6},{6,2},{3,7},{7,3},{8,13},{12,8},{9,1... | collective-permute-start | bytes 159752 | tf_op jit(solution)/shard_map/ppermute | solution.py:402
  87.6 4.3 %collective-permute-start.30 = (f32[2,104,128]{2,1,0:T(8,128)S(1)}, f32[2,104,128]{2,1,0:T(8,128)S(1)}, u32[]{:S(2)}, u32[]{:S(2)}) collective-permute-start(f32[2,104,128]{2,1,0:T(8,128)S(1)} %get-tuple-element.443), channel_id=1, source_target_pairs={{5,6},{9,10},{12,13},{14,15},{16,17},{18,19},{21,22},{24,25},{26,2... | collective-permute-start | bytes 319496 | tf_op jit(solution)/shard_map/ppermute | solution.py:420
  93.3 8.1 %collective-permute-start.31 = (f32[104,128]{1,0:T(8,128)S(1)}, f32[104,128]{1,0:T(8,128)S(1)}, u32[]{:S(2)}, u32[]{:S(2)}) collective-permute-start(f32[104,128]{1,0:T(8,128)S(1)} %get-tuple-element.452), channel_id=1, source_target_pairs={{0,4},{4,0},{1,5},{5,1},{2,6},{6,2},{3,7},{7,3},{8,12},{12,8},{9,1... | collective-permute-start | bytes 159752 | tf_op jit(solution)/shard_map/ppermute | solution.py:402
  104.5 8.4 %collective-permute-start.35 = (f32[104,128]{1,0:T(8,128)S(1)}, f32[104,128]{1,0:T(8,128)S(1)}, u32[]{:S(2)}, u32[]{:S(2)}) collective-permute-start(f32[104,128]{1,0:T(8,128)S(1)} %get-tuple-element.470), channel_id=1, source_target_pairs={{0,4},{4,0},{1,5},{5,1},{2,6},{6,2},{3,7},{7,3},{8,12},{12,9},{9,1... | collective-permute-start | bytes 159752 | tf_op jit(solution)/shard_map/ppermute | solution.py:402
  116.1 6.1 %collective-permute-start.39 = (f32[104,128]{1,0:T(8,128)S(1)}, f32[104,128]{1,0:T(8,128)S(1)}, u32[]{:S(2)}, u32[]{:S(2)}) collective-permute-start(f32[104,128]{1,0:T(8,128)S(1)} %get-tuple-element.488), channel_id=1, source_target_pairs={{0,4},{4,1},{1,5},{5,0},{2,6},{6,3},{3,7},{7,2},{8,12},{12,9},{9,1... | collective-permute-start | bytes 159752 | tf_op jit(solution)/shard_map/ppermute | solution.py:402
  120.0 5.1 %collective-permute-start.42 = (f32[2,104,128]{2,1,0:T(8,128)S(1)}, f32[2,104,128]{2,1,0:T(8,128)S(1)}, u32[]{:S(2)}, u32[]{:S(2)}) collective-permute-start(f32[2,104,128]{2,1,0:T(8,128)S(1)} %get-tuple-element.497), channel_id=1, source_target_pairs={{4,5},{6,7},{8,9},{10,11},{13,14},{17,18},{20,21},{22,23},{25,26},... | collective-permute-start | bytes 319496 | tf_op jit(solution)/shard_map/ppermute | solution.py:420
  125.3 7.6 %collective-permute-start.43 = (f32[104,128]{1,0:T(8,128)S(1)}, f32[104,128]{1,0:T(8,128)S(1)}, u32[]{:S(2)}, u32[]{:S(2)}) collective-permute-start(f32[104,128]{1,0:T(8,128)S(1)} %get-tuple-element.506), channel_id=1, source_target_pairs={{0,4},{4,0},{1,5},{5,1},{2,6},{6,2},{3,7},{7,3},{8,12},{12,9},{9,1... | collective-permute-start | bytes 159752 | tf_op jit(solution)/shard_map/ppermute | solution.py:402
  134.7 7.1 %collective-permute-start.47 = (f32[104,128]{1,0:T(8,128)S(1)}, f32[104,128]{1,0:T(8,128)S(1)}, u32[]{:S(2)}, u32[]{:S(2)}) collective-permute-start(f32[104,128]{1,0:T(8,128)S(1)} %get-tuple-element.524), channel_id=1, source_target_pairs={{0,4},{4,0},{1,5},{5,1},{2,6},{6,2},{3,7},{7,3},{8,12},{12,8},{9,1... | collective-permute-start | bytes 159752 | tf_op jit(solution)/shard_map/ppermute | solution.py:402
  139.7 5.0 %collective-permute-start.50 = (f32[2,104,128]{2,1,0:T(8,128)S(1)}, f32[2,104,128]{2,1,0:T(8,128)S(1)}, u32[]{:S(2)}, u32[]{:S(2)}) collective-permute-start(f32[2,104,128]{2,1,0:T(8,128)S(1)} %get-tuple-element.533), channel_id=1, source_target_pairs={{1,2},{5,6},{8,9},{10,11},{13,14},{17,18},{20,21},{22,23},{25,26},... | collective-permute-start | bytes 319496 | tf_op jit(solution)/shard_map/ppermute | solution.py:420
  145.0 6.2 %collective-permute-start.51 = (f32[104,128]{1,0:T(8,128)S(1)}, f32[104,128]{1,0:T(8,128)S(1)}, u32[]{:S(2)}, u32[]{:S(2)}) collective-permute-start(f32[104,128]{1,0:T(8,128)S(1)} %get-tuple-element.542), channel_id=1, source_target_pairs={{0,4},{4,0},{1,5},{5,1},{2,6},{6,2},{3,7},{7,3},{8,13},{12,8},{9,1... | collective-permute-start | bytes 159752 | tf_op jit(solution)/shard_map/ppermute | solution.py:402
  153.4 7.9 %collective-permute-start.55 = (f32[104,128]{1,0:T(8,128)S(1)}, f32[104,128]{1,0:T(8,128)S(1)}, u32[]{:S(2)}, u32[]{:S(2)}) collective-permute-start(f32[104,128]{1,0:T(8,128)S(1)} %get-tuple-element.560), channel_id=1, source_target_pairs={{0,5},{4,0},{1,4},{5,1},{2,7},{6,2},{3,6},{7,3},{8,13},{12,8},{9,1... | collective-permute-start | bytes 159752 | tf_op jit(solution)/shard_map/ppermute | solution.py:402
  158.1 4.3 %collective-permute-start.57 = (f32[2,104,128]{2,1,0:T(8,128)S(1)}, f32[2,104,128]{2,1,0:T(8,128)S(1)}, u32[]{:S(2)}, u32[]{:S(2)}) collective-permute-start(f32[2,104,128]{2,1,0:T(8,128)S(1)} %get-tuple-element.568), channel_id=1, source_target_pairs={{1,2},{8,9},{10,11},{20,21},{22,23},{2,1},{9,8},{11,10},{21,20},{2... | collective-permute-start | bytes 319496 | tf_op jit(solution)/shard_map/ppermute | solution.py:420
  163.5 8.3 %collective-permute-start.58 = (f32[104,128]{1,0:T(8,128)S(1)}, f32[104,128]{1,0:T(8,128)S(1)}, u32[]{:S(2)}, u32[]{:S(2)}) collective-permute-start(f32[104,128]{1,0:T(8,128)S(1)} %get-tuple-element.575), channel_id=1, source_target_pairs={{0,5},{4,0},{1,4},{5,1},{2,7},{6,2},{3,6},{7,3},{8,13},{12,8},{9,1... | collective-permute-start | bytes 159752 | tf_op jit(solution)/shard_map/ppermute | solution.py:402
  174.0 8.7 %collective-permute-start.60 = (f32[104,128]{1,0:T(8,128)S(1)}, f32[104,128]{1,0:T(8,128)S(1)}, u32[]{:S(2)}, u32[]{:S(2)}) collective-permute-start(f32[104,128]{1,0:T(8,128)S(1)} %get-tuple-element.585), channel_id=1, source_target_pairs={{0,5},{4,0},{1,4},{5,1},{2,7},{6,2},{3,6},{7,3},{8,13},{12,8},{9,1... | collective-permute-start | bytes 159752 | tf_op jit(solution)/shard_map/ppermute | solution.py:402
  184.9 7.9 %collective-permute-start.62 = (f32[104,128]{1,0:T(8,128)S(1)}, f32[104,128]{1,0:T(8,128)S(1)}, u32[]{:S(2)}, u32[]{:S(2)}) collective-permute-start(f32[104,128]{1,0:T(8,128)S(1)} %get-tuple-element.595), channel_id=1, source_target_pairs={{0,5},{4,0},{1,4},{5,1},{2,7},{6,2},{3,6},{7,3},{8,12},{12,8},{9,1... | collective-permute-start | bytes 159752 | tf_op jit(solution)/shard_map/ppermute | solution.py:402
  (39 other events, 79.4 us)

commit v4 on v3

--- a/solution.py
+++ b/solution.py
@@ -10,7 +10,7 @@
 SUBLANES = 8
 VMEM_LIMIT = 2 * 1024 * 1024
 PREPARE_LIMIT = 12 * 1024 * 1024
-LATERAL_START = 4
+LATERAL_START = 6
 CHUNKS = 4
 DIAG, UP, DOWN, LEFT, RIGHT = range(5)
 
@@ -369,8 +369,9 @@
     incoming = arrived = blank
     middle = size // 2 // SUBLANES * SUBLANES
     late_blocks = [(up_block, 0, UP, 0, size)]
-    for slot in (LEFT, RIGHT, DOWN):
+    for slot in (LEFT, RIGHT):
         late_blocks += [(side_blocks, slot - DOWN, slot, 0, middle), (side_blocks, slot - DOWN, slot, middle, size)]
+    late_blocks.append((side_blocks, 0, DOWN, 0, size))
 
     def tasks_at(tick):
         return [task_at(tick, place, count, vectors, lambda which, a, b: a if which else b) for place in range(count)]

time: 196 us -> 195 us (level)
    pallas_call x7 -> x6, Pallas kernels: 14.5 us -> 13.5 us  [later_call(): pl.pallas_call(functools.partial(later_kernel, face, slot, low, high), ou...]
    ppermute x26 -> x25, starting transfers between devices: 22.2 us -> 21.8 us  [per_device(): lax.ppermute(cross[0], ('sweep', 'span'), closed(pairs, range(count * par...]
    pallas_call x76 -> x75, Pallas kernels: 18.4 us -> 18.1 us  [call(): pl.pallas_call(body, out_shape=tuple((held(shape) for shape in [*(a.shape...]
  transfers between devices with their start and end apart: 63 -> 62, of which waited for: 26 -> 27; matrix products, arithmetic and copies ran while one was open for 0% -> 0% of each run, Pallas kernels for 13% -> 13%
where the time goes in v4:
time: 195 us; the launch traced here: 194 us
  starting transfers between devices  126 us (65%)
  Pallas kernels  34.8 us (18%)
  waiting for transfers between devices  31.9 us (16%)
    ppermute x37, starting transfers between devices, per_device(): incoming = lax.ppermute(value, ('sweep', 'span'), pairs)  104 us
    ppermute x37, waiting for transfers between devices, per_device(): incoming = lax.ppermute(value, ('sweep', 'span'), pairs)  31.9 us
    ppermute x25, starting transfers between devices, per_device(): lax.ppermute(cross[0], ('sweep', 'span'), closed(pairs, range(count * par...  21.8 us
    pallas_call x75, Pallas kernels, call(): pl.pallas_call(body, out_shape=tuple((held(shape) for shape in [*(a.shape...  18.1 us
    pallas_call x6, Pallas kernels, later_call(): pl.pallas_call(functools.partial(later_kernel, face, slot, low, high), ou...  13.5 us
  transfers between devices with their start and end apart: 62, of which 27 were waited for; matrix products, arithmetic and copies ran while one was open for 0% of the time, Pallas kernels for 13%

profile of v4, /device:TPU:0, one launch (start us, length us, event | category | flops | bytes accessed | tf_op | source)
XLA Modules:
  0.0 194.0 jit_solution(10387906034464138919)
XLA Ops:
  0.0 3.2 %first.1 = (f32[5,100,104,128]{3,2,1,0:T(8,128)S(1)}, f32[4,104,128]{2,1,0:T(8,128)S(1)}, f32[4,104,128]{2,1,0:T(8,128)S(1)}, f32[104,128]{1,0:T(8,128)S(1)}, s3...) custom-call(bf16[100,100,128]{2,1,0:T(8,128)(2,1)} %bitcast.10, ...), custom_call_target="tpu_custom_call" | custom-call | tf_op jit(solution)/shard_map/first/pallas_call | solution.py:311
  6.2 2.9 %later.6.refs_7_ = f32[5,100,104,128]{3,2,1,0:T(8,128)S(1)} custom-call(bf16[1,1,100,100,128]{4,3,2,1,0:T(8,128)(2,1)} %block.6, f32[5,100,104,128]{3,2,1,0:T(8,128)S(1)} %get-tuple-element.311.blocks_in), custom_call_target="tpu_custom_call", output_to_operand_aliasing={{}: (1, {})} | custom-call | tf_op jit(solution)/shard_map/later/pallas_call | solution.py:328
  11.5 4.2 %collective-permute-start.2 = (f32[104,128]{1,0:T(8,128)S(1)}, f32[104,128]{1,0:T(8,128)S(1)}, u32[]{:S(2)}, u32[]{:S(2)}) collective-permute-start(f32[104,128]{1,0:T(8,128)S(1)} %get-tuple-element.320), channel_id=1, source_target_pairs={{0,4},{4,1},{1,5},{5,0},{2,6},{6,3},{3,7},{7,2},{8,12},{12,9},{9,1... | collective-permute-start | bytes 159752 | tf_op jit(solution)/shard_map/ppermute | solution.py:403
  20.2 5.1 %collective-permute-start.4 = (f32[104,128]{1,0:T(8,128)S(1)}, f32[104,128]{1,0:T(8,128)S(1)}, u32[]{:S(2)}, u32[]{:S(2)}) collective-permute-start(f32[104,128]{1,0:T(8,128)S(1)} %get-tuple-element.330), channel_id=1, source_target_pairs={{0,4},{4,1},{1,5},{5,0},{2,6},{6,3},{3,7},{7,2},{8,12},{12,9},{9,1... | collective-permute-start | bytes 159752 | tf_op jit(solution)/shard_map/ppermute | solution.py:403
  27.4 2.9 %later.11.refs_7_ = f32[5,100,104,128]{3,2,1,0:T(8,128)S(1)} custom-call(bf16[1,1,3,100,100,128]{5,4,3,2,1,0:T(8,128)(2,1)} %block.11, f32[5,100,104,128]{3,2,1,0:T(8,128)S(1)} %get-tuple-element.336.blocks_in), custom_call_target="tpu_custom_call", output_to_operand_aliasing={{}: (1, {})} | custom-call | tf_op jit(solution)/shard_map/later/pallas_call | solution.py:328
  30.7 4.1 %collective-permute-start.6 = (f32[104,128]{1,0:T(8,128)S(1)}, f32[104,128]{1,0:T(8,128)S(1)}, u32[]{:S(2)}, u32[]{:S(2)}) collective-permute-start(f32[104,128]{1,0:T(8,128)S(1)} %get-tuple-element.340), channel_id=1, source_target_pairs={{0,4},{4,1},{1,5},{5,0},{2,6},{6,3},{3,7},{7,2},{8,12},{12,9},{9,1... | collective-permute-start | bytes 159752 | tf_op jit(solution)/shard_map/ppermute | solution.py:403
  37.9 6.5 %collective-permute-start.10 = (f32[104,128]{1,0:T(8,128)S(1)}, f32[104,128]{1,0:T(8,128)S(1)}, u32[]{:S(2)}, u32[]{:S(2)}) collective-permute-start(f32[104,128]{1,0:T(8,128)S(1)} %get-tuple-element.356), channel_id=1, source_target_pairs={{0,4},{4,0},{1,5},{5,1},{2,6},{6,2},{3,7},{7,3},{8,12},{12,9},{9,1... | collective-permute-start | bytes 159752 | tf_op jit(solution)/shard_map/ppermute | solution.py:403
  48.8 5.1 %collective-permute-start.14 = (f32[104,128]{1,0:T(8,128)S(1)}, f32[104,128]{1,0:T(8,128)S(1)}, u32[]{:S(2)}, u32[]{:S(2)}) collective-permute-start(f32[104,128]{1,0:T(8,128)S(1)} %get-tuple-element.374), channel_id=1, source_target_pairs={{0,4},{4,0},{1,5},{5,1},{2,6},{6,2},{3,7},{7,3},{8,12},{12,8},{9,1... | collective-permute-start | bytes 159752 | tf_op jit(solution)/shard_map/ppermute | solution.py:403
  58.9 4.2 %collective-permute-start.18 = (f32[104,128]{1,0:T(8,128)S(1)}, f32[104,128]{1,0:T(8,128)S(1)}, u32[]{:S(2)}, u32[]{:S(2)}) collective-permute-start(f32[104,128]{1,0:T(8,128)S(1)} %get-tuple-element.392), channel_id=1, source_target_pairs={{0,4},{4,0},{1,5},{5,1},{2,6},{6,2},{3,7},{7,3},{8,13},{12,8},{9,1... | collective-permute-start | bytes 159752 | tf_op jit(solution)/shard_map/ppermute | solution.py:403
  67.4 7.2 %collective-permute-start.22 = (f32[104,128]{1,0:T(8,128)S(1)}, f32[104,128]{1,0:T(8,128)S(1)}, u32[]{:S(2)}, u32[]{:S(2)}) collective-permute-start(f32[104,128]{1,0:T(8,128)S(1)} %get-tuple-element.410), channel_id=1, source_target_pairs={{0,5},{4,0},{1,4},{5,1},{2,7},{6,2},{3,6},{7,3},{8,13},{12,8},{9,1... | collective-permute-start | bytes 159752 | tf_op jit(solution)/shard_map/ppermute | solution.py:403
  80.2 6.3 %collective-permute-start.26 = (f32[104,128]{1,0:T(8,128)S(1)}, f32[104,128]{1,0:T(8,128)S(1)}, u32[]{:S(2)}, u32[]{:S(2)}) collective-permute-start(f32[104,128]{1,0:T(8,128)S(1)} %get-tuple-element.428), channel_id=1, source_target_pairs={{0,4},{4,0},{1,5},{5,1},{2,6},{6,2},{3,7},{7,3},{8,13},{12,8},{9,1... | collective-permute-start | bytes 159752 | tf_op jit(solution)/shard_map/ppermute | solution.py:403
  92.0 5.7 %collective-permute-start.30 = (f32[104,128]{1,0:T(8,128)S(1)}, f32[104,128]{1,0:T(8,128)S(1)}, u32[]{:S(2)}, u32[]{:S(2)}) collective-permute-start(f32[104,128]{1,0:T(8,128)S(1)} %get-tuple-element.446), channel_id=1, source_target_pairs={{0,4},{4,0},{1,5},{5,1},{2,6},{6,2},{3,7},{7,3},{8,12},{12,8},{9,1... | collective-permute-start | bytes 159752 | tf_op jit(solution)/shard_map/ppermute | solution.py:403
  103.3 5.6 %collective-permute-start.34 = (f32[104,128]{1,0:T(8,128)S(1)}, f32[104,128]{1,0:T(8,128)S(1)}, u32[]{:S(2)}, u32[]{:S(2)}) collective-permute-start(f32[104,128]{1,0:T(8,128)S(1)} %get-tuple-element.464), channel_id=1, source_target_pairs={{0,4},{4,0},{1,5},{5,1},{2,6},{6,2},{3,7},{7,3},{8,12},{12,9},{9,1... | collective-permute-start | bytes 159752 | tf_op jit(solution)/shard_map/ppermute | solution.py:403
  114.5 4.0 %collective-permute-start.38 = (f32[104,128]{1,0:T(8,128)S(1)}, f32[104,128]{1,0:T(8,128)S(1)}, u32[]{:S(2)}, u32[]{:S(2)}) collective-permute-start(f32[104,128]{1,0:T(8,128)S(1)} %get-tuple-element.482), channel_id=1, source_target_pairs={{0,4},{4,1},{1,5},{5,0},{2,6},{6,3},{3,7},{7,2},{8,12},{12,9},{9,1... | collective-permute-start | bytes 159752 | tf_op jit(solution)/shard_map/ppermute | solution.py:403
  123.7 5.1 %collective-permute-start.42 = (f32[104,128]{1,0:T(8,128)S(1)}, f32[104,128]{1,0:T(8,128)S(1)}, u32[]{:S(2)}, u32[]{:S(2)}) collective-permute-start(f32[104,128]{1,0:T(8,128)S(1)} %get-tuple-element.500), channel_id=1, source_target_pairs={{0,4},{4,0},{1,5},{5,1},{2,6},{6,2},{3,7},{7,3},{8,12},{12,9},{9,1... | collective-permute-start | bytes 159752 | tf_op jit(solution)/shard_map/ppermute | solution.py:403
  133.1 5.0 %collective-permute-start.46 = (f32[104,128]{1,0:T(8,128)S(1)}, f32[104,128]{1,0:T(8,128)S(1)}, u32[]{:S(2)}, u32[]{:S(2)}) collective-permute-start(f32[104,128]{1,0:T(8,128)S(1)} %get-tuple-element.518), channel_id=1, source_target_pairs={{0,4},{4,0},{1,5},{5,1},{2,6},{6,2},{3,7},{7,3},{8,12},{12,8},{9,1... | collective-permute-start | bytes 159752 | tf_op jit(solution)/shard_map/ppermute | solution.py:403
  143.5 3.8 %collective-permute-start.50 = (f32[104,128]{1,0:T(8,128)S(1)}, f32[104,128]{1,0:T(8,128)S(1)}, u32[]{:S(2)}, u32[]{:S(2)}) collective-permute-start(f32[104,128]{1,0:T(8,128)S(1)} %get-tuple-element.536), channel_id=1, source_target_pairs={{0,4},{4,0},{1,5},{5,1},{2,6},{6,2},{3,7},{7,3},{8,13},{12,8},{9,1... | collective-permute-start | bytes 159752 | tf_op jit(solution)/shard_map/ppermute | solution.py:403
  151.6 4.4 %collective-permute-start.54 = (f32[104,128]{1,0:T(8,128)S(1)}, f32[104,128]{1,0:T(8,128)S(1)}, u32[]{:S(2)}, u32[]{:S(2)}) collective-permute-start(f32[104,128]{1,0:T(8,128)S(1)} %get-tuple-element.554), channel_id=1, source_target_pairs={{0,5},{4,0},{1,4},{5,1},{2,7},{6,2},{3,6},{7,3},{8,13},{12,8},{9,1... | collective-permute-start | bytes 159752 | tf_op jit(solution)/shard_map/ppermute | solution.py:403
  161.7 5.6 %collective-permute-start.57 = (f32[104,128]{1,0:T(8,128)S(1)}, f32[104,128]{1,0:T(8,128)S(1)}, u32[]{:S(2)}, u32[]{:S(2)}) collective-permute-start(f32[104,128]{1,0:T(8,128)S(1)} %get-tuple-element.569), channel_id=1, source_target_pairs={{0,5},{4,0},{1,4},{5,1},{2,7},{6,2},{3,6},{7,3},{8,13},{12,8},{9,1... | collective-permute-start | bytes 159752 | tf_op jit(solution)/shard_map/ppermute | solution.py:403
  167.3 3.1 %collective-permute-done.57.refs_5_ = f32[104,128]{1,0:T(8,128)S(1)} collective-permute-done((f32[104,128]{1,0:T(8,128)S(1)}, f32[104,128]{1,0:T(8,128)S(1)}, u32[]{:S(2)}, u32[]{:S(2)}) %collective-permute-start.57) | collective-permute-done | bytes 53280 | tf_op jit(solution)/shard_map/ppermute | solution.py:403
  172.5 5.9 %collective-permute-start.59 = (f32[104,128]{1,0:T(8,128)S(1)}, f32[104,128]{1,0:T(8,128)S(1)}, u32[]{:S(2)}, u32[]{:S(2)}) collective-permute-start(f32[104,128]{1,0:T(8,128)S(1)} %get-tuple-element.579), channel_id=1, source_target_pairs={{0,5},{4,0},{1,4},{5,1},{2,7},{6,2},{3,6},{7,3},{8,13},{12,8},{9,1... | collective-permute-start | bytes 159752 | tf_op jit(solution)/shard_map/ppermute | solution.py:403
  178.4 3.3 %collective-permute-done.59.refs_5_ = f32[104,128]{1,0:T(8,128)S(1)} collective-permute-done((f32[104,128]{1,0:T(8,128)S(1)}, f32[104,128]{1,0:T(8,128)S(1)}, u32[]{:S(2)}, u32[]{:S(2)}) %collective-permute-start.59) | collective-permute-done | bytes 53280 | tf_op jit(solution)/shard_map/ppermute | solution.py:403
  183.9 4.6 %collective-permute-start.61 = (f32[104,128]{1,0:T(8,128)S(1)}, f32[104,128]{1,0:T(8,128)S(1)}, u32[]{:S(2)}, u32[]{:S(2)}) collective-permute-start(f32[104,128]{1,0:T(8,128)S(1)} %get-tuple-element.589), channel_id=1, source_target_pairs={{0,5},{4,0},{1,4},{5,1},{2,7},{6,2},{3,6},{7,3},{8,12},{12,8},{9,1... | collective-permute-start | bytes 159752 | tf_op jit(solution)/shard_map/ppermute | solution.py:403
  188.5 3.3 %collective-permute-done.61.refs_5_ = f32[104,128]{1,0:T(8,128)S(1)} collective-permute-done((f32[104,128]{1,0:T(8,128)S(1)}, f32[104,128]{1,0:T(8,128)S(1)}, u32[]{:S(2)}, u32[]{:S(2)}) %collective-permute-start.61) | collective-permute-done | bytes 53280 | tf_op jit(solution)/shard_map/ppermute | solution.py:403
  (184 shorter events, 82.1 us)
Async XLA Ops:
  3.6 5.5 %collective-permute-start = (f32[104,128]{1,0:T(8,128)S(1)}, f32[104,128]{1,0:T(8,128)S(1)}, u32[]{:S(2)}, u32[]{:S(2)}) collective-permute-start(f32[104,128]{1,0:T(8,128)S(1)} %get-tuple-element.310), channel_id=1, source_target_pairs={{0,4},{4,1},{1,5},{5,0},{2,6},{6,3},{3,7},{7,2},{8,12},{12,8},{9,1... | collective-permute-start | bytes 159752 | tf_op jit(solution)/shard_map/ppermute | solution.py:403
  11.5 6.2 %collective-permute-start.2 = (f32[104,128]{1,0:T(8,128)S(1)}, f32[104,128]{1,0:T(8,128)S(1)}, u32[]{:S(2)}, u32[]{:S(2)}) collective-permute-start(f32[104,128]{1,0:T(8,128)S(1)} %get-tuple-element.320), channel_id=1, source_target_pairs={{0,4},{4,1},{1,5},{5,0},{2,6},{6,3},{3,7},{7,2},{8,12},{12,9},{9,1... | collective-permute-start | bytes 159752 | tf_op jit(solution)/shard_map/ppermute | solution.py:403
  20.2 7.1 %collective-permute-start.4 = (f32[104,128]{1,0:T(8,128)S(1)}, f32[104,128]{1,0:T(8,128)S(1)}, u32[]{:S(2)}, u32[]{:S(2)}) collective-permute-start(f32[104,128]{1,0:T(8,128)S(1)} %get-tuple-element.330), channel_id=1, source_target_pairs={{0,4},{4,1},{1,5},{5,0},{2,6},{6,3},{3,7},{7,2},{8,12},{12,9},{9,1... | collective-permute-start | bytes 159752 | tf_op jit(solution)/shard_map/ppermute | solution.py:403
  30.7 5.9 %collective-permute-start.6 = (f32[104,128]{1,0:T(8,128)S(1)}, f32[104,128]{1,0:T(8,128)S(1)}, u32[]{:S(2)}, u32[]{:S(2)}) collective-permute-start(f32[104,128]{1,0:T(8,128)S(1)} %get-tuple-element.340), channel_id=1, source_target_pairs={{0,4},{4,1},{1,5},{5,0},{2,6},{6,3},{3,7},{7,2},{8,12},{12,9},{9,1... | collective-permute-start | bytes 159752 | tf_op jit(solution)/shard_map/ppermute | solution.py:403
  37.9 8.7 %collective-permute-start.10 = (f32[104,128]{1,0:T(8,128)S(1)}, f32[104,128]{1,0:T(8,128)S(1)}, u32[]{:S(2)}, u32[]{:S(2)}) collective-permute-start(f32[104,128]{1,0:T(8,128)S(1)} %get-tuple-element.356), channel_id=1, source_target_pairs={{0,4},{4,0},{1,5},{5,1},{2,6},{6,2},{3,7},{7,3},{8,12},{12,9},{9,1... | collective-permute-start | bytes 159752 | tf_op jit(solution)/shard_map/ppermute | solution.py:403
  48.8 7.2 %collective-permute-start.14 = (f32[104,128]{1,0:T(8,128)S(1)}, f32[104,128]{1,0:T(8,128)S(1)}, u32[]{:S(2)}, u32[]{:S(2)}) collective-permute-start(f32[104,128]{1,0:T(8,128)S(1)} %get-tuple-element.374), channel_id=1, source_target_pairs={{0,4},{4,0},{1,5},{5,1},{2,6},{6,2},{3,7},{7,3},{8,12},{12,8},{9,1... | collective-permute-start | bytes 159752 | tf_op jit(solution)/shard_map/ppermute | solution.py:403
  53.8 4.8 %collective-permute-start.17 = (f32[2,104,128]{2,1,0:T(8,128)S(1)}, f32[2,104,128]{2,1,0:T(8,128)S(1)}, u32[]{:S(2)}, u32[]{:S(2)}) collective-permute-start(f32[2,104,128]{2,1,0:T(8,128)S(1)} %get-tuple-element.383), channel_id=1, source_target_pairs={{1,2},{4,5},{6,7},{8,9},{10,11},{12,13},{14,15},{16,17},{18,19},{2... | collective-permute-start | bytes 319496 | tf_op jit(solution)/shard_map/ppermute | solution.py:421
  58.9 6.3 %collective-permute-start.18 = (f32[104,128]{1,0:T(8,128)S(1)}, f32[104,128]{1,0:T(8,128)S(1)}, u32[]{:S(2)}, u32[]{:S(2)}) collective-permute-start(f32[104,128]{1,0:T(8,128)S(1)} %get-tuple-element.392), channel_id=1, source_target_pairs={{0,4},{4,0},{1,5},{5,1},{2,6},{6,2},{3,7},{7,3},{8,13},{12,8},{9,1... | collective-permute-start | bytes 159752 | tf_op jit(solution)/shard_map/ppermute | solution.py:403
  67.4 9.7 %collective-permute-start.22 = (f32[104,128]{1,0:T(8,128)S(1)}, f32[104,128]{1,0:T(8,128)S(1)}, u32[]{:S(2)}, u32[]{:S(2)}) collective-permute-start(f32[104,128]{1,0:T(8,128)S(1)} %get-tuple-element.410), channel_id=1, source_target_pairs={{0,5},{4,0},{1,4},{5,1},{2,7},{6,2},{3,6},{7,3},{8,13},{12,8},{9,1... | collective-permute-start | bytes 159752 | tf_op jit(solution)/shard_map/ppermute | solution.py:403
  80.2 8.6 %collective-permute-start.26 = (f32[104,128]{1,0:T(8,128)S(1)}, f32[104,128]{1,0:T(8,128)S(1)}, u32[]{:S(2)}, u32[]{:S(2)}) collective-permute-start(f32[104,128]{1,0:T(8,128)S(1)} %get-tuple-element.428), channel_id=1, source_target_pairs={{0,4},{4,0},{1,5},{5,1},{2,6},{6,2},{3,7},{7,3},{8,13},{12,8},{9,1... | collective-permute-start | bytes 159752 | tf_op jit(solution)/shard_map/ppermute | solution.py:403
  92.0 8.2 %collective-permute-start.30 = (f32[104,128]{1,0:T(8,128)S(1)}, f32[104,128]{1,0:T(8,128)S(1)}, u32[]{:S(2)}, u32[]{:S(2)}) collective-permute-start(f32[104,128]{1,0:T(8,128)S(1)} %get-tuple-element.446), channel_id=1, source_target_pairs={{0,4},{4,0},{1,5},{5,1},{2,6},{6,2},{3,7},{7,3},{8,12},{12,8},{9,1... | collective-permute-start | bytes 159752 | tf_op jit(solution)/shard_map/ppermute | solution.py:403
  97.6 4.3 %collective-permute-start.33 = (f32[2,104,128]{2,1,0:T(8,128)S(1)}, f32[2,104,128]{2,1,0:T(8,128)S(1)}, u32[]{:S(2)}, u32[]{:S(2)}) collective-permute-start(f32[2,104,128]{2,1,0:T(8,128)S(1)} %get-tuple-element.455), channel_id=1, source_target_pairs={{5,6},{8,9},{10,11},{12,13},{14,15},{16,17},{18,19},{20,21},{22,23... | collective-permute-start | bytes 319496 | tf_op jit(solution)/shard_map/ppermute | solution.py:421
  103.3 8.1 %collective-permute-start.34 = (f32[104,128]{1,0:T(8,128)S(1)}, f32[104,128]{1,0:T(8,128)S(1)}, u32[]{:S(2)}, u32[]{:S(2)}) collective-permute-start(f32[104,128]{1,0:T(8,128)S(1)} %get-tuple-element.464), channel_id=1, source_target_pairs={{0,4},{4,0},{1,5},{5,1},{2,6},{6,2},{3,7},{7,3},{8,12},{12,9},{9,1... | collective-permute-start | bytes 159752 | tf_op jit(solution)/shard_map/ppermute | solution.py:403
  114.5 6.2 %collective-permute-start.38 = (f32[104,128]{1,0:T(8,128)S(1)}, f32[104,128]{1,0:T(8,128)S(1)}, u32[]{:S(2)}, u32[]{:S(2)}) collective-permute-start(f32[104,128]{1,0:T(8,128)S(1)} %get-tuple-element.482), channel_id=1, source_target_pairs={{0,4},{4,1},{1,5},{5,0},{2,6},{6,3},{3,7},{7,2},{8,12},{12,9},{9,1... | collective-permute-start | bytes 159752 | tf_op jit(solution)/shard_map/ppermute | solution.py:403
  118.5 5.0 %collective-permute-start.41 = (f32[2,104,128]{2,1,0:T(8,128)S(1)}, f32[2,104,128]{2,1,0:T(8,128)S(1)}, u32[]{:S(2)}, u32[]{:S(2)}) collective-permute-start(f32[2,104,128]{2,1,0:T(8,128)S(1)} %get-tuple-element.491), channel_id=1, source_target_pairs={{4,5},{6,7},{8,9},{10,11},{12,13},{14,15},{16,17},{18,19},{20,21},... | collective-permute-start | bytes 319496 | tf_op jit(solution)/shard_map/ppermute | solution.py:421
  123.7 7.6 %collective-permute-start.42 = (f32[104,128]{1,0:T(8,128)S(1)}, f32[104,128]{1,0:T(8,128)S(1)}, u32[]{:S(2)}, u32[]{:S(2)}) collective-permute-start(f32[104,128]{1,0:T(8,128)S(1)} %get-tuple-element.500), channel_id=1, source_target_pairs={{0,4},{4,0},{1,5},{5,1},{2,6},{6,2},{3,7},{7,3},{8,12},{12,9},{9,1... | collective-permute-start | bytes 159752 | tf_op jit(solution)/shard_map/ppermute | solution.py:403
  133.1 7.2 %collective-permute-start.46 = (f32[104,128]{1,0:T(8,128)S(1)}, f32[104,128]{1,0:T(8,128)S(1)}, u32[]{:S(2)}, u32[]{:S(2)}) collective-permute-start(f32[104,128]{1,0:T(8,128)S(1)} %get-tuple-element.518), channel_id=1, source_target_pairs={{0,4},{4,0},{1,5},{5,1},{2,6},{6,2},{3,7},{7,3},{8,12},{12,8},{9,1... | collective-permute-start | bytes 159752 | tf_op jit(solution)/shard_map/ppermute | solution.py:403
  138.1 5.1 %collective-permute-start.49 = (f32[2,104,128]{2,1,0:T(8,128)S(1)}, f32[2,104,128]{2,1,0:T(8,128)S(1)}, u32[]{:S(2)}, u32[]{:S(2)}) collective-permute-start(f32[2,104,128]{2,1,0:T(8,128)S(1)} %get-tuple-element.527), channel_id=1, source_target_pairs={{1,2},{5,6},{8,9},{10,11},{12,13},{14,15},{16,17},{18,19},{20,21},... | collective-permute-start | bytes 319496 | tf_op jit(solution)/shard_map/ppermute | solution.py:421
  143.5 6.2 %collective-permute-start.50 = (f32[104,128]{1,0:T(8,128)S(1)}, f32[104,128]{1,0:T(8,128)S(1)}, u32[]{:S(2)}, u32[]{:S(2)}) collective-permute-start(f32[104,128]{1,0:T(8,128)S(1)} %get-tuple-element.536), channel_id=1, source_target_pairs={{0,4},{4,0},{1,5},{5,1},{2,6},{6,2},{3,7},{7,3},{8,13},{12,8},{9,1... | collective-permute-start | bytes 159752 | tf_op jit(solution)/shard_map/ppermute | solution.py:403
  151.6 7.9 %collective-permute-start.54 = (f32[104,128]{1,0:T(8,128)S(1)}, f32[104,128]{1,0:T(8,128)S(1)}, u32[]{:S(2)}, u32[]{:S(2)}) collective-permute-start(f32[104,128]{1,0:T(8,128)S(1)} %get-tuple-element.554), channel_id=1, source_target_pairs={{0,5},{4,0},{1,4},{5,1},{2,7},{6,2},{3,6},{7,3},{8,13},{12,8},{9,1... | collective-permute-start | bytes 159752 | tf_op jit(solution)/shard_map/ppermute | solution.py:403
  156.0 4.8 %collective-permute-start.56 = (f32[2,104,128]{2,1,0:T(8,128)S(1)}, f32[2,104,128]{2,1,0:T(8,128)S(1)}, u32[]{:S(2)}, u32[]{:S(2)}) collective-permute-start(f32[2,104,128]{2,1,0:T(8,128)S(1)} %get-tuple-element.562), channel_id=1, source_target_pairs={{1,2},{8,9},{10,11},{20,21},{22,23},{2,1},{9,8},{11,10},{21,20},{2... | collective-permute-start | bytes 319496 | tf_op jit(solution)/shard_map/ppermute | solution.py:421
  161.7 8.6 %collective-permute-start.57 = (f32[104,128]{1,0:T(8,128)S(1)}, f32[104,128]{1,0:T(8,128)S(1)}, u32[]{:S(2)}, u32[]{:S(2)}) collective-permute-start(f32[104,128]{1,0:T(8,128)S(1)} %get-tuple-element.569), channel_id=1, source_target_pairs={{0,5},{4,0},{1,4},{5,1},{2,7},{6,2},{3,6},{7,3},{8,13},{12,8},{9,1... | collective-permute-start | bytes 159752 | tf_op jit(solution)/shard_map/ppermute | solution.py:403
  172.5 9.2 %collective-permute-start.59 = (f32[104,128]{1,0:T(8,128)S(1)}, f32[104,128]{1,0:T(8,128)S(1)}, u32[]{:S(2)}, u32[]{:S(2)}) collective-permute-start(f32[104,128]{1,0:T(8,128)S(1)} %get-tuple-element.579), channel_id=1, source_target_pairs={{0,5},{4,0},{1,4},{5,1},{2,7},{6,2},{3,6},{7,3},{8,13},{12,8},{9,1... | collective-permute-start | bytes 159752 | tf_op jit(solution)/shard_map/ppermute | solution.py:403
  183.9 7.9 %collective-permute-start.61 = (f32[104,128]{1,0:T(8,128)S(1)}, f32[104,128]{1,0:T(8,128)S(1)}, u32[]{:S(2)}, u32[]{:S(2)}) collective-permute-start(f32[104,128]{1,0:T(8,128)S(1)} %get-tuple-element.589), channel_id=1, source_target_pairs={{0,5},{4,0},{1,4},{5,1},{2,7},{6,2},{3,6},{7,3},{8,12},{12,8},{9,1... | collective-permute-start | bytes 159752 | tf_op jit(solution)/shard_map/ppermute | solution.py:403
  (38 other events, 78.8 us)
